TPU v7x, 128 devices: a whole 4x4x4 slice. The times are simulated.
128 devices in a mesh: sec: 2 (over core), row: 8 (over x, z_lo), nest: 8 (over y, z_hi).
Axes of the slice: x: 4, y: 4, z: 4 (z_hi: 2, z_lo: 2; z = z_hi * 2 + z_lo), core: 2. Of those that a mesh axis runs over, the one named last changes fastest.
Arguments:
- ocean_state: float32 [2, 3, 512, 1024], P('sec', None, 'row', 'nest'), may hold values from -1.2 to 1.2
- face_depth: float32 [2, 2, 512, 1024], P('sec', None, 'row', 'nest'), may hold values from 2 to 4
- face_open: int32 [2, 2, 512, 1024], P('sec', None, 'row', 'nest'), may hold values 0 or 1
- nest_place: int32 [64], replicated, may hold values from 0 to 383, as said below
- nest_host: int32 [64], replicated, may hold values from 0 to 127, as said below
Outputs:
- final_state: float32 [2, 3, 512, 1024], P('sec', None, 'row', 'nest')
Inputs may be any that keep to these rules, and one draw needn't show every extreme that they name: `nest_place`: distinct positions; the first and the last position are always covered. `nest_host`: distinct slots; both slots of some device hold a nest; the nest at the first position lives in the last slot and the nest at the last position in the first slot.
All inputs are finite; a program needn't handle non-finite values. No bound on the sum of `face_open` on one device may be relied on, other than what follows from the above.
Results may differ from a plain program's by a relative error of at most 0.00013.
Values sent between devices are 32-bit elements; how exact they have to be, the bound alone decides.
No kernel may reach another device: no remote copies, remote signals or barrier semaphores. Data moves between devices by JAX's collectives and lax.ppermute only.
A program may use at most 64 MiB of HBM per device.

v0:
```python
import jax
import jax.numpy as jnp
from jax import lax
from jax.experimental import pallas as pl
from jax.experimental.pallas import tpu as pltpu
from jax.sharding import PartitionSpec as P

PH = 8
PW = 32
RR = 4
K = 2
STEPS = 4
NESTS = 64
COURANT = 0.3

ROWS = 64
COLS = 128
FR = RR * PH
SPOTS = RR - 1
PEERS = 64
HALO = 4
EXT = ROWS + 2 * HALO
TOP = (RR - 1) * PH // 2
LEFT = PW // 2
CHAN = 7
UNIT = 4
UNITS = 8
BLOCK = UNIT * UNITS
HALO_ROW = 6 * UNIT
EDGE_ROW = 7 * UNIT

VMEM = pl.BlockSpec(memory_space=pltpu.VMEM)
SMEM = pl.BlockSpec(memory_space=pltpu.SMEM)


def div6(p):
    return (p * 10923) >> 16


def div3(p):
    return (p * 21846) >> 16


def channel(state_ref, depth_ref, open_ref, k, rows):
    if k < 3:
        return state_ref[0, k, rows, :]
    if k < 5:
        return depth_ref[0, k - 3, rows, :]
    return open_ref[0, k - 5, rows, :].astype(jnp.float32)


def pack_kernel(state_ref, depth_ref, open_ref, out_ref):
    for b in range(K):
        rows = pl.ds(b * FR, FR)
        for k in range(8):
            start = (k // UNIT) * FR * 8 + b * UNIT + k % UNIT
            if k < CHAN:
                value = channel(state_ref, depth_ref, open_ref, k, rows)
            else:
                value = jnp.zeros((FR, COLS), jnp.float32)
            out_ref[pl.ds(start, FR, stride=8), :] = value


def compact_kernel(place_ref, host_ref, own_ref, other_ref, out_ref, table_ref):
    sec = lax.axis_index("sec")
    me = lax.axis_index("row") * lax.axis_size("nest") + lax.axis_index("nest")
    upper = lax.broadcasted_iota(jnp.int32, (8, COLS), 0) >= UNIT

    def copy(source_ref, unit_from, dest, unit_to):
        piece = source_ref[pl.ds(pl.multiple_of((unit_from >> 1) * 8, 8), 8), :]
        swap = (unit_from & 1) != (unit_to & 1)
        piece = jnp.where(swap, pltpu.roll(piece, UNIT, 0), piece)
        spot = pl.ds(pl.multiple_of(dest * BLOCK + (unit_to >> 1) * 8, 8), 8)
        out_ref[spot, :] = jnp.where(upper == ((unit_to & 1) == 1), piece, out_ref[spot, :])

    out_ref[...] = jnp.zeros_like(out_ref)

    @pl.when(sec == 0)
    def _():
        def place_one(n, carry):
            p = place_ref[n]
            t = div6(p)
            copy(other_ref, host_ref[n], t, p - 6 * t)
            return carry

        lax.fori_loop(0, NESTS, place_one, 0, unroll=4)

        tile = lax.broadcasted_iota(jnp.int32, (PEERS, COLS), 0)
        lane = lax.broadcasted_iota(jnp.int32, (PEERS, COLS), 1)
        tile_col = tile & 7
        from_right = (lane < HALO) & (tile_col < 7)
        from_left = (lane >= COLS - HALO) & (tile_col > 0)

        def edges(x):
            right = pltpu.roll(x, PEERS - 1, 0)
            left = pltpu.roll(x, 1, 0)
            return jnp.where(from_right, right, jnp.where(from_left, left, 0.0))

        below = (me & (FR - 1)) < FR // 2
        packed = jnp.zeros((PEERS, COLS), jnp.float32)
        for c in range(UNIT):
            band0 = own_ref[pl.ds(c, PEERS, stride=8), :]
            band1 = own_ref[pl.ds(UNIT + c, PEERS, stride=8), :]
            packed += pltpu.roll(edges(band0), HALO + 8 * c, 1)
            packed += pltpu.roll(edges(band1), HALO + 8 * (UNIT + c), 1)
            down = jnp.where(tile < PEERS - 8, pltpu.roll(band0, PEERS - 8, 0), 0.0)
            up = jnp.where(tile >= 8, pltpu.roll(band1, 8, 0), 0.0)
            vertical = jnp.where(below, down, up)
            packed += pltpu.roll(edges(vertical), HALO + 8 * (2 * UNIT + c), 1)
            out_ref[pl.ds(HALO_ROW + c, PEERS, stride=BLOCK), :] = vertical
        out_ref[pl.ds(EDGE_ROW, PEERS, stride=BLOCK), :] = packed

    @pl.when(sec == 1)
    def _():
        def clear(n, carry):
            base = 3 * div3(place_ref[n])
            for j in range(SPOTS):
                table_ref[base + j] = 0
            return carry

        def note(n, carry):
            table_ref[place_ref[n]] = host_ref[n]
            return carry

        def gather_band(n, carry):
            p = place_ref[n]
            h = host_ref[n]
            dest = h >> 1
            unit = (h & 1) * UNIT
            band = div3(p)
            copy(other_ref, band, dest, unit)
            for j in range(SPOTS):
                copy(own_ref, table_ref[3 * band + j], dest, unit + 1 + j)
            return carry

        lax.fori_loop(0, NESTS, clear, 0, unroll=4)
        lax.fori_loop(0, NESTS, note, 0, unroll=4)
        lax.fori_loop(0, NESTS, gather_band, 0, unroll=2)


def window_kernel(
    place_ref, host_ref, state_ref, depth_ref, open_ref, got_ref, out_ref,
    outer_ref, fine_ref, rep_ref, cov_ref, at_ref,
):
    sec = lax.axis_index("sec")
    row = lax.axis_index("row")
    col = lax.axis_index("nest")
    row_count = lax.axis_size("row")
    col_count = lax.axis_size("nest")
    me = row * col_count + col

    def got(k, unit_row, rows=FR, first=0):
        start = ((k // UNIT) * FR + first) * BLOCK + unit_row + k % UNIT
        return got_ref[pl.ds(start, rows, stride=BLOCK), :]

    for u in range(6):
        cov_ref[u] = 0
    at_ref[0] = -1
    at_ref[1] = -1

    @pl.when(sec == 0)
    def _():
        def scan(n, carry):
            p = place_ref[n]
            t = div6(p)

            @pl.when(t == me)
            def _():
                cov_ref[p - 6 * t] = 1

            return carry

        lax.fori_loop(0, NESTS, scan, 0, unroll=4)
        lane = lax.broadcasted_iota(jnp.int32, (FR, COLS), 1)
        keep = (lane < HALO) | (lane >= COLS - HALO)
        for k in range(CHAN):
            for b in range(K):
                for j in range(SPOTS):
                    fine_ref[3 * b + j, k] = got(k, UNIT * (3 * b + j))
                outer_ref[k, pl.ds(HALO + b * FR, FR), 0:COLS] = channel(
                    state_ref, depth_ref, open_ref, k, pl.ds(b * FR, FR)
                )
            outer_ref[k, 0:HALO, 0:COLS] = got(k, HALO_ROW, HALO, FR - HALO)
            outer_ref[k, EXT - HALO : EXT, 0:COLS] = got(k, HALO_ROW, HALO, 0)
        for g in range(2):
            start = g * FR * BLOCK + EDGE_ROW
            packed = got_ref[pl.ds(start, FR, stride=BLOCK), :]
            for c in range(UNIT):
                k = g * UNIT + c
                if k >= CHAN:
                    continue
                for b in range(K):
                    shift = HALO + 8 * (b * UNIT + c)
                    side = jnp.where(keep, pltpu.roll(packed, COLS - shift, 1), 0.0)
                    outer_ref[k, pl.ds(HALO + b * FR, FR), COLS : 2 * COLS] = side
                shift = HALO + 8 * (2 * UNIT + c)
                side = jnp.where(keep, pltpu.roll(packed, COLS - shift, 1), 0.0)
                outer_ref[k, 0:HALO, COLS : 2 * COLS] = side[FR - HALO :]
                outer_ref[k, EXT - HALO : EXT, COLS : 2 * COLS] = side[:HALO]

    @pl.when(sec == 1)
    def _():
        def find(n, carry):
            h = host_ref[n]

            @pl.when((h >> 1) == me)
            def _():
                at_ref[h & 1] = place_ref[n]

            return carry

        lax.fori_loop(0, NESTS, find, 0, unroll=4)
        bands = [div3(at_ref[s]) for s in range(K)]

        def scan(n, carry):
            p = place_ref[n]
            band = div3(p)
            for s in range(K):

                @pl.when((at_ref[s] >= 0) & (band == bands[s]))
                def _():
                    cov_ref[3 * s + p - 3 * band] = 1

            return carry

        lax.fori_loop(0, NESTS, scan, 0, unroll=4)
        for k in range(CHAN):
            outer_ref[k] = jnp.zeros((EXT, 2 * COLS), jnp.float32)
            for s in range(K):
                outer_ref[k, pl.ds(HALO + s * FR, FR), 0:COLS] = got(k, UNIT * UNIT * s)
                for j in range(SPOTS):
                    fine_ref[3 * s + j, k] = got(k, UNIT * (UNIT * s + 1 + j))

    ext_row = lax.broadcasted_iota(jnp.int32, (EXT, 2 * COLS), 0)
    ext_lane = lax.broadcasted_iota(jnp.int32, (EXT, 2 * COLS), 1)
    row_low = jnp.where((sec == 0) & (row == 0), HALO, 0)
    row_high = jnp.where((sec == 0) & (row == row_count - 1), EXT - HALO, EXT)
    right_end = jnp.where((sec == 0) & (col < col_count - 1), COLS + HALO, COLS)
    left_start = jnp.where((sec == 0) & (col > 0), 2 * COLS - HALO, 2 * COLS)
    inside = (
        (ext_row >= row_low)
        & (ext_row < row_high)
        & ((ext_lane < right_end) | (ext_lane >= left_start))
    )

    small_lane = lax.broadcasted_iota(jnp.int32, (PH, COLS), 1)
    lane = lax.broadcasted_iota(jnp.int32, (FR, COLS), 1)
    fine_row = lax.broadcasted_iota(jnp.int32, (FR, COLS), 0)
    spread = [LEFT + PW * j + (small_lane >> 2) for j in range(SPOTS)]
    gathered = [
        jnp.clip(RR * (small_lane - LEFT - PW * j), 0, COLS - RR) for j in range(SPOTS)
    ]
    mine = [
        (small_lane >= LEFT + PW * j) & (small_lane < LEFT + PW * (j + 1)) for j in range(SPOTS)
    ]

    def take(x, index):
        return jnp.take_along_axis(x, index, axis=1, mode="promise_in_bounds")

    def ghosts(surface, eastward, southward, slot):
        ends = []
        for b in range(K):
            r0 = HALO + TOP + b * FR
            e_rows = eastward[r0 : r0 + PH, :COLS]
            s_rows = surface[r0 : r0 + PH, :COLS]
            north = jnp.broadcast_to(southward[r0 - 1 : r0, :COLS], (PH, COLS))
            south = jnp.broadcast_to(surface[r0 + PH : r0 + PH + 1, :COLS], (PH, COLS))
            for j in range(SPOTS):
                c0 = LEFT + PW * j
                west = pltpu.roll(e_rows, COLS - (c0 - 1), 1)
                east = pltpu.roll(s_rows, COLS - 1 - (c0 + PW), 1)
                side = jnp.where(small_lane == 0, west, east)
                for i in range(RR):
                    rep_ref[slot, 3 * b + j, pl.ds(i, PH, stride=RR), :] = side
                ends.append((take(north, spread[j]), take(south, spread[j])))
        return ends

    def tall(x):
        return jnp.concatenate([x] * RR, axis=0)

    old_ends = ghosts(outer_ref[0], outer_ref[1], outer_ref[2], 0)
    for step in range(STEPS):
        old, new = step % 2, (step + 1) % 2
        surface, eastward, southward = outer_ref[0], outer_ref[1], outer_ref[2]
        flow = (eastward - pltpu.roll(eastward, 1, 1)) + (southward - pltpu.roll(southward, 1, 0))
        surface = jnp.where(inside, surface - COURANT * flow, 0.0)
        to_east = pltpu.roll(surface, 2 * COLS - 1, 1)
        to_south = pltpu.roll(surface, EXT - 1, 0)
        eastward = outer_ref[5] * (
            eastward - COURANT * (outer_ref[3] + 0.5 * (surface + to_east)) * (to_east - surface)
        )
        southward = outer_ref[6] * (
            southward - COURANT * (outer_ref[4] + 0.5 * (surface + to_south)) * (to_south - surface)
        )
        outer_ref[0] = surface
        outer_ref[1] = eastward
        outer_ref[2] = southward
        new_ends = ghosts(surface, eastward, southward, new)
        for nest in range(K * SPOTS):
            b, j = nest // SPOTS, nest % SPOTS
            level, east_flux, south_flux = (fine_ref[nest, k] for k in range(3))
            old_side, new_side = rep_ref[old, nest], rep_ref[new, nest]
            (old_north, old_south), (new_north, new_south) = old_ends[nest], new_ends[nest]
            for m in range(1, RR + 1):
                part = m / RR
                side = old_side + part * (new_side - old_side)
                north = tall(old_north + part * (new_north - old_north))
                south = tall(old_south + part * (new_south - old_south))
                west_of = jnp.where(lane == 0, side, pltpu.roll(east_flux, 1, 1))
                north_of = jnp.where(fine_row == 0, north, pltpu.roll(south_flux, 1, 0))
                level = level - COURANT * ((east_flux - west_of) + (south_flux - north_of))
                east_of = jnp.where(lane == COLS - 1, side, pltpu.roll(level, COLS - 1, 1))
                south_of = jnp.where(fine_row == FR - 1, south, pltpu.roll(level, FR - 1, 0))
                east_flux = fine_ref[nest, 5] * (
                    east_flux
                    - COURANT * (fine_ref[nest, 3] + 0.5 * (level + east_of)) * (east_of - level)
                )
                south_flux = fine_ref[nest, 6] * (
                    south_flux
                    - COURANT * (fine_ref[nest, 4] + 0.5 * (level + south_of)) * (south_of - level)
                )
            for k, value in enumerate((level, east_flux, south_flux)):
                fine_ref[nest, k] = value

            def every(k, i):
                return fine_ref[nest, k, pl.ds(i, PH, stride=RR), :]

            def quads(x):
                x = x + pltpu.roll(x, COLS - 1, 1)
                return x + pltpu.roll(x, COLS - 2, 1)

            mean_level = quads((every(0, 0) + every(0, 1)) + (every(0, 2) + every(0, 3)))
            mean_east = (every(1, 0) + every(1, 1)) + (every(1, 2) + every(1, 3))
            mean_south = quads(every(2, RR - 1))
            back = (
                take(mean_level, gathered[j]) * (1.0 / (RR * RR)),
                take(mean_east, gathered[j] + (RR - 1)) * (1.0 / RR),
                take(mean_south, gathered[j]) * (1.0 / RR),
            )
            here = mine[j] & (cov_ref[nest] == 1)
            rows = pl.ds(HALO + TOP + b * FR, PH)
            for k in range(3):
                outer_ref[k, rows, 0:COLS] = jnp.where(here, back[k], outer_ref[k, rows, 0:COLS])
        old_ends = new_ends

    @pl.when(sec == 0)
    def _():
        for k in range(3):
            out_ref[0, k] = outer_ref[k, HALO : HALO + ROWS, 0:COLS]

    @pl.when(sec == 1)
    def _():
        for s in range(K):
            p = at_ref[s]
            j = jnp.where(p >= 0, p - 3 * div3(p), 0)
            for k in range(3):
                rows = pl.ds(s * FR, FR)
                out_ref[0, k, rows, :] = jnp.where(
                    p >= 0, fine_ref[3 * s + j, k], state_ref[0, k, rows, :]
                )


def on_device(ocean_state, face_depth, face_open, nest_place, nest_host):
    tiles = ("row", "nest")
    packed = pl.pallas_call(
        pack_kernel,
        out_shape=jax.ShapeDtypeStruct((PEERS * 8, COLS), jnp.float32),
        in_specs=[VMEM, VMEM, VMEM],
        out_specs=VMEM,
        name="pack",
    )(ocean_state, face_depth, face_open)
    pieces = lax.all_to_all(
        packed.reshape(PEERS, 8, COLS), tiles, split_axis=0, concat_axis=0, tiled=True
    )
    others = lax.ppermute(pieces, "sec", [(0, 1), (1, 0)])
    blocks = pl.pallas_call(
        compact_kernel,
        out_shape=jax.ShapeDtypeStruct((PEERS * BLOCK, COLS), jnp.float32),
        in_specs=[SMEM, SMEM, VMEM, VMEM],
        out_specs=VMEM,
        scratch_shapes=[pltpu.SMEM((PEERS * K * SPOTS,), jnp.int32)],
        name="compact",
    )(nest_place, nest_host, pieces.reshape(-1, COLS), others.reshape(-1, COLS))
    got = lax.all_to_all(
        blocks.reshape(PEERS, BLOCK, COLS), tiles, split_axis=0, concat_axis=0, tiled=True
    )
    return pl.pallas_call(
        window_kernel,
        out_shape=jax.ShapeDtypeStruct(ocean_state.shape, jnp.float32),
        in_specs=[SMEM, SMEM, VMEM, VMEM, VMEM, VMEM],
        out_specs=VMEM,
        scratch_shapes=[
            pltpu.VMEM((CHAN, EXT, 2 * COLS), jnp.float32),
            pltpu.VMEM((K * SPOTS, CHAN, FR, COLS), jnp.float32),
            pltpu.VMEM((2, K * SPOTS, FR, COLS), jnp.float32),
            pltpu.SMEM((K * SPOTS,), jnp.int32),
            pltpu.SMEM((K,), jnp.int32),
        ],
        compiler_params=pltpu.CompilerParams(vmem_limit_bytes=32 * 1024 * 1024),
        name="window",
    )(nest_place, nest_host, ocean_state, face_depth, face_open, got.reshape(-1, COLS))


def solution(mesh):
    placed = (
        P("sec", None, "row", "nest"),
        P("sec", None, "row", "nest"),
        P("sec", None, "row", "nest"),
        P(),
        P(),
    )
    return jax.shard_map(
        on_device,
        mesh=mesh,
        in_specs=placed,
        out_specs=P("sec", None, "row", "nest"),
        check_vma=False,
    )
```

profile of v0, /device:TPU:1, one launch (start us, length us, event | category | flops | bytes accessed | tf_op | source)
XLA Modules:
  0.0 61.9 jit_solution(11313079696767562783)
XLA Ops:
  0.0 1.7 %pack.1 = f32[512,128]{1,0:T(8,128)} custom-call(f32[1,3,64,128]{3,2,1,0:T(8,128)} %state_ref.3, f32[1,2,64,128]{3,2,1,0:T(8,128)} %depth_ref.3, s32[1,2,64,128]{3,2,1,0:T(8,128)} %open_ref.3), custom_call_target="tpu_custom_call" | custom-call | tf_op jit(solution)/shard_map/pack/pallas_call | solution.py:365
  1.7 21.4 %all_to_all.10 = f32[64,8,128]{2,1,0:T(8,128)S(1)} all-to-all(f32[64,8,128]{2,1,0:T(8,128)} %bitcast.7), channel_id=1, replica_groups=mesh['sec'=2,'row'=8,'nest'=8] {'row','nest'}, dimensions={0} | all-to-all | bytes 524288 | tf_op jit(solution)/shard_map/all_to_all | solution.py:372
  23.0 0.0 copy-start.5
  23.0 2.1 %collective-permute-start = (f32[64,8,128]{2,1,0:T(8,128)S(1)}, f32[64,8,128]{2,1,0:T(8,128)S(1)}, u32[]{:S(2)}, u32[]{:S(2)}) collective-permute-start(f32[64,8,128]{2,1,0:T(8,128)S(1)} %all_to_all.10), channel_id=1, source_target_pairs={{0,64},{64,0},{1,65},{65,1},{2,66},{66,2},{3,67},{67,3},{4,68},{68... | collective-permute-start | bytes 786440 | tf_op jit(solution)/shard_map/ppermute | solution.py:375
  25.1 1.2 %collective-permute-done = f32[64,8,128]{2,1,0:T(8,128)S(1)} collective-permute-done((f32[64,8,128]{2,1,0:T(8,128)S(1)}, f32[64,8,128]{2,1,0:T(8,128)S(1)}, u32[]{:S(2)}, u32[]{:S(2)}) %collective-permute-start) | collective-permute-done | bytes 262176 | tf_op jit(solution)/shard_map/ppermute | solution.py:375
  26.3 0.0 copy-start.6
  26.3 0.0 copy-done.5
  26.3 0.7 %copy-done.6 = f32[64,8,128]{2,1,0:T(8,128)} copy-done((f32[64,8,128]{2,1,0:T(8,128)}, f32[64,8,128]{2,1,0:T(8,128)S(1)}, u32[]{:S(2)}) %copy-start.6) | copy-done | bytes 262168
  27.0 4.0 %compact.1 = f32[2048,128]{1,0:T(8,128)} custom-call(s32[64]{0:T(128)} %place_ref.3, s32[64]{0:T(128)} %host_ref.3, f32[512,128]{1,0:T(8,128)} %bitcast.8, f32[512,128]{1,0:T(8,128)} %bitcast.9), custom_call_target="tpu_custom_call" | custom-call | tf_op jit(solution)/shard_map/compact/pallas_call | solution.py:376
  30.9 0.0 copy-start
  30.9 0.0 copy-start.1
  30.9 0.0 copy-start.2
  30.9 24.0 %all_to_all.11 = f32[64,32,128]{2,1,0:T(8,128)S(1)} all-to-all(f32[64,32,128]{2,1,0:T(8,128)} %bitcast.6), channel_id=1, replica_groups=mesh['sec'=2,'row'=8,'nest'=8] {'row','nest'}, dimensions={0} | all-to-all | bytes 2097152 | tf_op jit(solution)/shard_map/all_to_all | solution.py:384
  54.9 0.0 copy-start.3
  54.9 0.0 copy-start.4
  54.9 0.0 copy-done
  54.9 0.0 copy-done.1
  54.9 0.0 copy-done.2
  55.0 0.6 %copy-done.3 = s32[64]{0:T(128)S(1)} copy-done((s32[64]{0:T(128)S(1)}, s32[64]{0:T(128)}, u32[]{:S(2)}) %copy-start.3) | copy-done | bytes 280
  55.6 0.0 copy-done.4
  55.6 6.3 %window.1 = f32[1,3,64,128]{3,2,1,0:T(8,128)} custom-call(s32[64]{0:T(128)S(1)} %copy-done.3, s32[64]{0:T(128)S(1)} %copy-done.4, f32[1,3,64,128]{3,2,1,0:T(8,128)S(1)} %copy-done, f32[1,2,64,128]{3,2,1,0:T(8,128)S(1)} %copy-done.1, s32[1,2,64,128]{3,2,1,0:T(8,128)S(1)} %copy-done.2, f32[2048,128]{1,0:T(8,128)S(1)} %bitcast.5), custom_call_target="tpu_custom_call" | custom-call | tf_op jit(solution)/shard_map/window/pallas_call | solution.py:387
Async XLA Ops:
  23.0 3.2 %copy-start.5 = (f32[64,8,128]{2,1,0:T(8,128)}, f32[64,8,128]{2,1,0:T(8,128)S(1)}, u32[]{:S(2)}) copy-start(f32[64,8,128]{2,1,0:T(8,128)S(1)} %all_to_all.10) | copy-start | bytes 786436
  23.0 3.2 %collective-permute-start = (f32[64,8,128]{2,1,0:T(8,128)S(1)}, f32[64,8,128]{2,1,0:T(8,128)S(1)}, u32[]{:S(2)}, u32[]{:S(2)}) collective-permute-start(f32[64,8,128]{2,1,0:T(8,128)S(1)} %all_to_all.10), channel_id=1, source_target_pairs={{0,64},{64,0},{1,65},{65,1},{2,66},{66,2},{3,67},{67,3},{4,68},{68... | collective-permute-start | bytes 786440 | tf_op jit(solution)/shard_map/ppermute | solution.py:375
  26.3 0.7 %copy-start.6 = (f32[64,8,128]{2,1,0:T(8,128)}, f32[64,8,128]{2,1,0:T(8,128)S(1)}, u32[]{:S(2)}) copy-start(f32[64,8,128]{2,1,0:T(8,128)S(1)} %collective-permute-done) | copy-start | bytes 786436
  30.9 24.0 %copy-start = (f32[1,3,64,128]{3,2,1,0:T(8,128)S(1)}, f32[1,3,64,128]{3,2,1,0:T(8,128)}, u32[]{:S(2)}) copy-start(f32[1,3,64,128]{3,2,1,0:T(8,128)} %state_ref.3) | copy-start | bytes 294916
  30.9 24.0 %copy-start.1 = (f32[1,2,64,128]{3,2,1,0:T(8,128)S(1)}, f32[1,2,64,128]{3,2,1,0:T(8,128)}, u32[]{:S(2)}) copy-start(f32[1,2,64,128]{3,2,1,0:T(8,128)} %depth_ref.3) | copy-start | bytes 196612
  30.9 24.0 %copy-start.2 = (s32[1,2,64,128]{3,2,1,0:T(8,128)S(1)}, s32[1,2,64,128]{3,2,1,0:T(8,128)}, u32[]{:S(2)}) copy-start(s32[1,2,64,128]{3,2,1,0:T(8,128)} %open_ref.3) | copy-start | bytes 196612
  54.9 0.7 %copy-start.3 = (s32[64]{0:T(128)S(1)}, s32[64]{0:T(128)}, u32[]{:S(2)}) copy-start(s32[64]{0:T(128)} %place_ref.3) | copy-start | bytes 772
  54.9 0.7 %copy-start.4 = (s32[64]{0:T(128)S(1)}, s32[64]{0:T(128)}, u32[]{:S(2)}) copy-start(s32[64]{0:T(128)} %host_ref.3) | copy-start | bytes 772
where the time goes:
time: 62.2 us; the launch traced here: 61.9 us
  blocking collectives  45.4 us (73%)
  Pallas kernels  11.9 us (19%)
  starting transfers between devices  2.07 us (3%)
  local copies, waits for them, and re-layouts  1.35 us (2%)
  waiting for transfers between devices  1.16 us (2%)
    all_to_all x1, blocking collectives, on_device(): lax.all_to_all(blocks.reshape(PEERS, BLOCK, COLS), tiles, split_axis=0, c...  24 us
    all_to_all x1, blocking collectives, on_device(): lax.all_to_all(packed.reshape(PEERS, 8, COLS), tiles, split_axis=0, conca...  21.4 us
    pallas_call x1, Pallas kernels, on_device(): pl.pallas_call(window_kernel, out_shape=jax.ShapeDtypeStruct(ocean_state....  6.29 us
    pallas_call x1, Pallas kernels, on_device(): pl.pallas_call(compact_kernel, out_shape=jax.ShapeDtypeStruct((PEERS * BL...  3.97 us
    ppermute x1, starting transfers between devices, on_device(): others = lax.ppermute(pieces, 'sec', [(0, 1), (1, 0)])  2.07 us
    pallas_call x1, Pallas kernels, on_device(): pl.pallas_call(pack_kernel, out_shape=jax.ShapeDtypeStruct((PEERS * 8, CO...  1.67 us
    unnamed x14, local copies, waits for them, and re-layouts  1.35 us
  transfers between devices with their start and end apart: 1, of which 1 were waited for; matrix products, arithmetic and copies ran while one was open for 0% of the time, Pallas kernels for 0%

commit v1 on v0

--- a/solution.py
+++ b/solution.py
@@ -24,10 +24,11 @@
 LEFT = PW // 2
 CHAN = 7
 UNIT = 4
-UNITS = 8
+UNITS = 6
 BLOCK = UNIT * UNITS
-HALO_ROW = 6 * UNIT
-EDGE_ROW = 7 * UNIT
+HALF = COLS // 2
+LAST = CHAN - 1
+PART = LAST // 2
 
 VMEM = pl.BlockSpec(memory_space=pltpu.VMEM)
 SMEM = pl.BlockSpec(memory_space=pltpu.SMEM)
@@ -41,37 +42,68 @@
     return (p * 21846) >> 16
 
 
-def channel(state_ref, depth_ref, open_ref, k, rows):
-    if k < 3:
-        return state_ref[0, k, rows, :]
-    if k < 5:
-        return depth_ref[0, k - 3, rows, :]
-    return open_ref[0, k - 5, rows, :].astype(jnp.float32)
-
-
-def pack_kernel(state_ref, depth_ref, open_ref, out_ref):
+def pack_kernel(
+    place_in, host_in, state_in, depth_in, open_in,
+    out_ref, place_ref, host_ref, state_ref, depth_ref, open_ref, sems,
+):
+    moves = [
+        pltpu.make_async_copy(source, target, sems.at[i])
+        for i, (source, target) in enumerate(
+            (
+                (state_in, state_ref), (depth_in, depth_ref), (open_in, open_ref),
+                (place_in, place_ref), (host_in, host_ref),
+            )
+        )
+    ]
+    for move in moves:
+        move.start()
+    for move in moves:
+        move.wait()
+
+    def channel(k, rows):
+        if k < 3:
+            return state_ref[0, k, rows, :]
+        if k < 5:
+            return depth_ref[0, k - 3, rows, :]
+        return open_ref[0, k - 5, rows, :].astype(jnp.float32)
+
+    first = lax.broadcasted_iota(jnp.int32, (8, COLS), 0) < HALO
+    rims = [
+        jnp.where(first, channel(k, pl.ds(0, 8)), channel(k, pl.ds(ROWS - 8, 8)))
+        for k in range(CHAN)
+    ]
+    rims = jnp.concatenate(rims + [jnp.zeros((8, COLS), jnp.float32)], axis=0)
+    left = lax.broadcasted_iota(jnp.int32, (FR, COLS), 1) < HALF
     for b in range(K):
         rows = pl.ds(b * FR, FR)
-        for k in range(8):
-            start = (k // UNIT) * FR * 8 + b * UNIT + k % UNIT
-            if k < CHAN:
-                value = channel(state_ref, depth_ref, open_ref, k, rows)
-            else:
-                value = jnp.zeros((FR, COLS), jnp.float32)
-            out_ref[pl.ds(start, FR, stride=8), :] = value
+        for g in range(2):
+            base = g * FR * 8 + b * UNIT
+            for c in range(PART):
+                out_ref[pl.ds(base + c, FR, stride=8), :] = channel(PART * g + c, rows)
+            half = channel(LAST, rows)
+            rim = rims[g * FR : (g + 1) * FR]
+            if g == 1:
+                half = pltpu.roll(half, HALF, 1)
+            if b == 0:
+                rim = pltpu.roll(rim, HALF, 1)
+            out_ref[pl.ds(base + PART, FR, stride=8), :] = jnp.where(left, half, rim)
 
 
 def compact_kernel(place_ref, host_ref, own_ref, other_ref, out_ref, table_ref):
     sec = lax.axis_index("sec")
     me = lax.axis_index("row") * lax.axis_size("nest") + lax.axis_index("nest")
-    upper = lax.broadcasted_iota(jnp.int32, (8, COLS), 0) >= UNIT
+    sub = lax.broadcasted_iota(jnp.int32, (8, COLS), 0)
+    sub_lane = lax.broadcasted_iota(jnp.int32, (8, COLS), 1)
+    used = (sub_lane < HALF) | ((sub & (UNIT - 1)) < PART)
+    halves = (used & (sub < UNIT), used & (sub >= UNIT))
 
     def copy(source_ref, unit_from, dest, unit_to):
         piece = source_ref[pl.ds(pl.multiple_of((unit_from >> 1) * 8, 8), 8), :]
         swap = (unit_from & 1) != (unit_to & 1)
         piece = jnp.where(swap, pltpu.roll(piece, UNIT, 0), piece)
         spot = pl.ds(pl.multiple_of(dest * BLOCK + (unit_to >> 1) * 8, 8), 8)
-        out_ref[spot, :] = jnp.where(upper == ((unit_to & 1) == 1), piece, out_ref[spot, :])
+        mask = jnp.where((unit_to & 1) == 1, halves[1].astype(jnp.int32), halves[0].astype(jnp.int32))
+        pltpu.store(out_ref.at[spot, :], piece, mask=mask == 1)
 
     out_ref[...] = jnp.zeros_like(out_ref)
 
@@ -83,32 +115,59 @@
             copy(other_ref, host_ref[n], t, p - 6 * t)
             return carry
 
-        lax.fori_loop(0, NESTS, place_one, 0, unroll=4)
+        lax.fori_loop(0, NESTS, place_one, 0, unroll=8)
 
         tile = lax.broadcasted_iota(jnp.int32, (PEERS, COLS), 0)
         lane = lax.broadcasted_iota(jnp.int32, (PEERS, COLS), 1)
         tile_col = tile & 7
-        from_right = (lane < HALO) & (tile_col < 7)
-        from_left = (lane >= COLS - HALO) & (tile_col > 0)
-
-        def edges(x):
-            right = pltpu.roll(x, PEERS - 1, 0)
-            left = pltpu.roll(x, 1, 0)
-            return jnp.where(from_right, right, jnp.where(from_left, left, 0.0))
-
-        below = (me & (FR - 1)) < FR // 2
+        has_right, has_left = tile_col < 7, tile_col > 0
+        lower_half = me < FR
+        to_above = ((me >> 2) & 1) == 0
+
+        def right_of(x):
+            return pltpu.roll(x, PEERS - 1, 0)
+
+        def left_of(x):
+            return pltpu.roll(x, 1, 0)
+
+        def row_of(i):
+            return own_ref[pl.ds(i, PEERS, stride=8), :]
+
         packed = jnp.zeros((PEERS, COLS), jnp.float32)
-        for c in range(UNIT):
-            band0 = own_ref[pl.ds(c, PEERS, stride=8), :]
-            band1 = own_ref[pl.ds(UNIT + c, PEERS, stride=8), :]
-            packed += pltpu.roll(edges(band0), HALO + 8 * c, 1)
-            packed += pltpu.roll(edges(band1), HALO + 8 * (UNIT + c), 1)
-            down = jnp.where(tile < PEERS - 8, pltpu.roll(band0, PEERS - 8, 0), 0.0)
-            up = jnp.where(tile >= 8, pltpu.roll(band1, 8, 0), 0.0)
-            vertical = jnp.where(below, down, up)
-            packed += pltpu.roll(edges(vertical), HALO + 8 * (2 * UNIT + c), 1)
-            out_ref[pl.ds(HALO_ROW + c, PEERS, stride=BLOCK), :] = vertical
-        out_ref[pl.ds(EDGE_ROW, PEERS, stride=BLOCK), :] = packed
+        rims = []
+        for b in range(K):
+            for c in range(PART):
+                x = row_of(UNIT * b + c)
+                side = jnp.where(
+                    has_right & (lane < HALO),
+                    right_of(x),
+                    jnp.where(has_left & (lane >= COLS - HALO), left_of(x), 0.0),
+                )
+                packed += pltpu.roll(side, HALF + HALO + 8 * (PART * b + c), 1)
+            x = row_of(UNIT * b + PART)
+            right = jnp.where(has_right & (lane < HALO), right_of(x), 0.0)
+            left = jnp.where(
+                has_left & (lane >= HALF - HALO) & (lane < HALF), left_of(x), 0.0
+            )
+            spot = HALF + 8 * PART * K + HALO * b
+            packed += jnp.where(
+                lower_half, pltpu.roll(right, spot, 1), pltpu.roll(left, spot - HALF + HALO, 1)
+            )
+            rims.append(
+                jnp.where(
+                    to_above,
+                    jnp.where(tile < PEERS - 8, pltpu.roll(x, PEERS - 8, 0), 0.0),
+                    jnp.where(tile >= 8, pltpu.roll(x, 8, 0), 0.0),
+                )
+            )
+        right = jnp.where(
+            has_right & (lane >= HALF) & (lane < HALF + HALO), right_of(rims[0]), 0.0
+        )
+        left = jnp.where(has_left & (lane >= COLS - HALO), left_of(rims[1]), 0.0)
+        packed += pltpu.roll(right, HALF - HALO, 1) + pltpu.roll(left, COLS - HALO, 1)
+        for u, value in enumerate([packed] + rims):
+            spot = pl.ds(UNIT * u + PART, PEERS, stride=BLOCK)
+            out_ref[spot, :] = jnp.where(lane >= HALF, value, out_ref[spot, :])
 
     @pl.when(sec == 1)
     def _():
@@ -126,16 +185,17 @@
             p = place_ref[n]
             h = host_ref[n]
             dest = h >> 1
-            unit = (h & 1) * UNIT
+            unit = (h & 1) * SPOTS
             band = div3(p)
+            j = p - 3 * band
             copy(other_ref, band, dest, unit)
-            for j in range(SPOTS):
-                copy(own_ref, table_ref[3 * band + j], dest, unit + 1 + j)
-            return carry
-
-        lax.fori_loop(0, NESTS, clear, 0, unroll=4)
-        lax.fori_loop(0, NESTS, note, 0, unroll=4)
-        lax.fori_loop(0, NESTS, gather_band, 0, unroll=2)
+            copy(own_ref, table_ref[3 * band + jnp.where(j == 0, 1, 0)], dest, unit + 1)
+            copy(own_ref, table_ref[3 * band + jnp.where(j == 2, 1, 2)], dest, unit + 2)
+            return carry
+
+        lax.fori_loop(0, NESTS, clear, 0, unroll=8)
+        lax.fori_loop(0, NESTS, note, 0, unroll=8)
+        lax.fori_loop(0, NESTS, gather_band, 0, unroll=4)
 
 
 def window_kernel(
@@ -148,10 +208,24 @@
     row_count = lax.axis_size("row")
     col_count = lax.axis_size("nest")
     me = row * col_count + col
-
-    def got(k, unit_row, rows=FR, first=0):
-        start = ((k // UNIT) * FR + first) * BLOCK + unit_row + k % UNIT
-        return got_ref[pl.ds(start, rows, stride=BLOCK), :]
+    lane = lax.broadcasted_iota(jnp.int32, (FR, COLS), 1)
+    small_lane = lax.broadcasted_iota(jnp.int32, (PH, COLS), 1)
+
+    def own(k, rows):
+        if k < 3:
+            return state_ref[0, k, rows, :]
+        if k < 5:
+            return depth_ref[0, k - 3, rows, :]
+        return open_ref[0, k - 5, rows, :].astype(jnp.float32)
+
+    def rows_of(peer, row, count):
+        return got_ref[pl.ds(peer * BLOCK + row, count, stride=BLOCK), :]
+
+    def got(k, unit):
+        if k < LAST:
+            return rows_of((k // PART) * FR, UNIT * unit + k % PART, FR)
+        left, right = (rows_of(g * FR, UNIT * unit + PART, FR) for g in range(2))
+        return jnp.where(lane < HALF, left, pltpu.roll(right, HALF, 1))
 
     for u in range(6):
         cov_ref[u] = 0
@@ -171,32 +245,35 @@
             return carry
 
         lax.fori_loop(0, NESTS, scan, 0, unroll=4)
-        lane = lax.broadcasted_iota(jnp.int32, (FR, COLS), 1)
         keep = (lane < HALO) | (lane >= COLS - HALO)
+        small_keep = (small_lane < HALO) | (small_lane >= COLS - HALO)
+        beside = [rows_of(g * FR, PART, FR) for g in range(2)]
         for k in range(CHAN):
             for b in range(K):
+                rows = pl.ds(HALO + b * FR, FR)
                 for j in range(SPOTS):
-                    fine_ref[3 * b + j, k] = got(k, UNIT * (3 * b + j))
-                outer_ref[k, pl.ds(HALO + b * FR, FR), 0:COLS] = channel(
-                    state_ref, depth_ref, open_ref, k, pl.ds(b * FR, FR)
-                )
-            outer_ref[k, 0:HALO, 0:COLS] = got(k, HALO_ROW, HALO, FR - HALO)
-            outer_ref[k, EXT - HALO : EXT, 0:COLS] = got(k, HALO_ROW, HALO, 0)
-        for g in range(2):
-            start = g * FR * BLOCK + EDGE_ROW
-            packed = got_ref[pl.ds(start, FR, stride=BLOCK), :]
-            for c in range(UNIT):
-                k = g * UNIT + c
-                if k >= CHAN:
-                    continue
-                for b in range(K):
-                    shift = HALO + 8 * (b * UNIT + c)
-                    side = jnp.where(keep, pltpu.roll(packed, COLS - shift, 1), 0.0)
-                    outer_ref[k, pl.ds(HALO + b * FR, FR), COLS : 2 * COLS] = side
-                shift = HALO + 8 * (2 * UNIT + c)
-                side = jnp.where(keep, pltpu.roll(packed, COLS - shift, 1), 0.0)
-                outer_ref[k, 0:HALO, COLS : 2 * COLS] = side[FR - HALO :]
-                outer_ref[k, EXT - HALO : EXT, COLS : 2 * COLS] = side[:HALO]
+                    fine_ref[3 * b + j, k] = got(k, 3 * b + j)
+                outer_ref[k, rows, 0:COLS] = own(k, pl.ds(b * FR, FR))
+                if k < LAST:
+                    shift = HALF + HALO + 8 * (PART * b + k % PART)
+                    side = pltpu.roll(beside[k // PART], COLS - shift, 1)
+                else:
+                    shift = HALF + 8 * PART * K + HALO * b
+                    side = jnp.where(
+                        lane < HALO,
+                        pltpu.roll(beside[0], COLS - shift, 1),
+                        pltpu.roll(beside[1], COLS - HALO - shift, 1),
+                    )
+                outer_ref[k, rows, COLS : 2 * COLS] = jnp.where(keep, side, 0.0)
+            rim = jnp.where(
+                small_lane < HALF,
+                pltpu.roll(rows_of(8 * k, UNIT + PART, 8), HALF, 1),
+                rows_of(8 * k, 2 * UNIT + PART, 8),
+            )
+            corner = jnp.where(small_keep, pltpu.roll(rows_of(8 * k, PART, 8), HALO, 1), 0.0)
+            for columns, value in ((pl.ds(0, COLS), rim), (pl.ds(COLS, COLS), corner)):
+                outer_ref[k, EXT - HALO : EXT, columns] = value[:HALO]
+                outer_ref[k, 0:HALO, columns] = value[HALO:]
 
     @pl.when(sec == 1)
     def _():
@@ -224,12 +301,18 @@
             return carry
 
         lax.fori_loop(0, NESTS, scan, 0, unroll=4)
+        for s in range(K):
+            j = jnp.where(at_ref[s] >= 0, at_ref[s] - 3 * bands[s], 0)
+            spots = (j, jnp.where(j == 0, 1, 0), jnp.where(j == 2, 1, 2))
+            for k in range(CHAN):
+                outer_ref[k, pl.ds(HALO + s * FR, FR), 0:COLS] = got(k, SPOTS * s)
+                fine_ref[3 * s + spots[0], k] = own(k, pl.ds(s * FR, FR))
+                fine_ref[3 * s + spots[1], k] = got(k, SPOTS * s + 1)
+                fine_ref[3 * s + spots[2], k] = got(k, SPOTS * s + 2)
         for k in range(CHAN):
-            outer_ref[k] = jnp.zeros((EXT, 2 * COLS), jnp.float32)
-            for s in range(K):
-                outer_ref[k, pl.ds(HALO + s * FR, FR), 0:COLS] = got(k, UNIT * UNIT * s)
-                for j in range(SPOTS):
-                    fine_ref[3 * s + j, k] = got(k, UNIT * (UNIT * s + 1 + j))
+            outer_ref[k, 0:HALO, 0:COLS] = jnp.zeros((HALO, COLS), jnp.float32)
+            outer_ref[k, EXT - HALO : EXT, 0:COLS] = jnp.zeros((HALO, COLS), jnp.float32)
+            outer_ref[k, :, COLS : 2 * COLS] = jnp.zeros((EXT, COLS), jnp.float32)
 
     ext_row = lax.broadcasted_iota(jnp.int32, (EXT, 2 * COLS), 0)
     ext_lane = lax.broadcasted_iota(jnp.int32, (EXT, 2 * COLS), 1)
@@ -243,8 +326,6 @@
         & ((ext_lane < right_end) | (ext_lane >= left_start))
     )
 
-    small_lane = lax.broadcasted_iota(jnp.int32, (PH, COLS), 1)
-    lane = lax.broadcasted_iota(jnp.int32, (FR, COLS), 1)
     fine_row = lax.broadcasted_iota(jnp.int32, (FR, COLS), 0)
     spread = [LEFT + PW * j + (small_lane >> 2) for j in range(SPOTS)]
     gathered = [
@@ -362,13 +443,27 @@
 
 def on_device(ocean_state, face_depth, face_open, nest_place, nest_host):
     tiles = ("row", "nest")
-    packed = pl.pallas_call(
+    packed, place, host = pl.pallas_call(
         pack_kernel,
-        out_shape=jax.ShapeDtypeStruct((PEERS * 8, COLS), jnp.float32),
-        in_specs=[VMEM, VMEM, VMEM],
-        out_specs=VMEM,
+        out_shape=(
+            jax.ShapeDtypeStruct((PEERS * 8, COLS), jnp.float32),
+            jax.ShapeDtypeStruct(nest_place.shape, jnp.int32),
+            jax.ShapeDtypeStruct(nest_host.shape, jnp.int32),
+        ),
+        in_specs=[pl.BlockSpec(memory_space=pltpu.HBM)] * 5,
+        out_specs=(VMEM, VMEM, VMEM),
+        scratch_shapes=[
+            pltpu.VMEM(ocean_state.shape, jnp.float32),
+            pltpu.VMEM(face_depth.shape, jnp.float32),
+            pltpu.VMEM(face_open.shape, jnp.int32),
+            pltpu.SemaphoreType.DMA((5,)),
+        ],
+        compiler_params=pltpu.CompilerParams(vmem_limit_bytes=4 * 1024 * 1024),
         name="pack",
-    )(ocean_state, face_depth, face_open)
+    )(*(
+        pltpu.with_memory_space_constraint(x, pltpu.HBM)
+        for x in (nest_place, nest_host, ocean_state, face_depth, face_open)
+    ))
     pieces = lax.all_to_all(
         packed.reshape(PEERS, 8, COLS), tiles, split_axis=0, concat_axis=0, tiled=True
     )
@@ -379,8 +474,9 @@
         in_specs=[SMEM, SMEM, VMEM, VMEM],
         out_specs=VMEM,
         scratch_shapes=[pltpu.SMEM((PEERS * K * SPOTS,), jnp.int32)],
+        compiler_params=pltpu.CompilerParams(vmem_limit_bytes=8 * 1024 * 1024),
         name="compact",
-    )(nest_place, nest_host, pieces.reshape(-1, COLS), others.reshape(-1, COLS))
+    )(place, host, pieces.reshape(-1, COLS), others.reshape(-1, COLS))
     got = lax.all_to_all(
         blocks.reshape(PEERS, BLOCK, COLS), tiles, split_axis=0, concat_axis=0, tiled=True
     )
@@ -398,7 +494,7 @@
         ],
         compiler_params=pltpu.CompilerParams(vmem_limit_bytes=32 * 1024 * 1024),
         name="window",
-    )(nest_place, nest_host, ocean_state, face_depth, face_open, got.reshape(-1, COLS))
+    )(place, host, ocean_state, face_depth, face_open, got.reshape(-1, COLS))
 
 
 def solution(mesh):

time: 62.2 us -> 54.5 us (0.88)
  the two profiles are of different devices: /device:TPU:1 before, /device:TPU:0 now
where the time goes in v1:
time: 54.5 us; the launch traced here: 53.5 us
  blocking collectives  44.1 us (81%)
  Pallas kernels  7.79 us (14%)
  waiting for transfers between devices  1.53 us (3%)
    all_to_all x1, blocking collectives, on_device(): lax.all_to_all(blocks.reshape(PEERS, BLOCK, COLS), tiles, split_axis=0, c...  22.3 us
    all_to_all x1, blocking collectives, on_device(): lax.all_to_all(packed.reshape(PEERS, 8, COLS), tiles, split_axis=0, conca...  21.8 us
    pallas_call x1, Pallas kernels, on_device(): pl.pallas_call(window_kernel, out_shape=jax.ShapeDtypeStruct(ocean_state....  5.55 us
    ppermute x1, waiting for transfers between devices, on_device(): others = lax.ppermute(pieces, 'sec', [(0, 1), (1, 0)])  1.53 us
    pallas_call x1, Pallas kernels, on_device(): pl.pallas_call(compact_kernel, out_shape=jax.ShapeDtypeStruct((PEERS * BL...  1.17 us
  transfers between devices with their start and end apart: 1, of which 1 were waited for; matrix products, arithmetic and copies ran while one was open for 0% of the time, Pallas kernels for 0%

profile of v1, /device:TPU:0, one launch (start us, length us, event | category | flops | bytes accessed | tf_op | source)
XLA Modules:
  0.0 53.5 jit_solution(2608608691499086263)
XLA Ops:
  0.0 1.1 %pack.1 = (f32[512,128]{1,0:T(8,128)S(1)}, s32[64]{0:T(128)S(1)}, s32[64]{0:T(128)S(1)}) custom-call(s32[64]{0:T(128)} %place_in.1, s32[64]{0:T(128)} %host_in.1, f32[1,3,64,128]{3,2,1,0:T(8,128)} %state_ref.1, f32[1,2,64,128]{3,2,1,0:T(8,128)} %depth_ref.1, s32[1,2,64,128]{3,2,1,0:T(8,128)} %open_ref.1), custom_call_target="tpu_custom_call" | custom-call | tf_op jit(solution)/shard_map/pack/pallas_call | solution.py:446
  1.1 21.8 %all_to_all.10 = f32[64,8,128]{2,1,0:T(8,128)S(1)} all-to-all(f32[64,8,128]{2,1,0:T(8,128)S(1)} %bitcast.8), channel_id=1, replica_groups=mesh['sec'=2,'row'=8,'nest'=8] {'row','nest'}, dimensions={0} | all-to-all | bytes 524288 | tf_op jit(solution)/shard_map/all_to_all | solution.py:467
  22.9 0.0 collective-permute-start
  22.9 1.5 %collective-permute-done = f32[64,8,128]{2,1,0:T(8,128)S(1)} collective-permute-done((f32[64,8,128]{2,1,0:T(8,128)S(1)}, f32[64,8,128]{2,1,0:T(8,128)S(1)}, u32[]{:S(2)}, u32[]{:S(2)}) %collective-permute-start) | collective-permute-done | bytes 262176 | tf_op jit(solution)/shard_map/ppermute | solution.py:470
  24.4 1.2 %compact.1 = f32[1536,128]{1,0:T(8,128)S(1)} custom-call(s32[64]{0:T(128)S(1)} %get-tuple-element.8.place_ref, s32[64]{0:T(128)S(1)} %get-tuple-element.9.host_ref, f32[512,128]{1,0:T(8,128)S(1)} %bitcast.7, f32[512,128]{1,0:T(8,128)S(1)} %bitcast.9), custom_call_target="tpu_custom_call" | custom-call | tf_op jit(solution)/shard_map/compact/pallas_call | solution.py:471
  25.6 0.0 copy-start
  25.6 0.0 copy-start.1
  25.6 0.0 copy-start.2
  25.6 22.3 %all_to_all.11 = f32[64,24,128]{2,1,0:T(8,128)S(1)} all-to-all(f32[64,24,128]{2,1,0:T(8,128)S(1)} %bitcast.6), channel_id=1, replica_groups=mesh['sec'=2,'row'=8,'nest'=8] {'row','nest'}, dimensions={0} | all-to-all | bytes 1572864 | tf_op jit(solution)/shard_map/all_to_all | solution.py:480
  47.9 0.0 copy-done
  47.9 0.0 copy-done.1
  47.9 0.0 copy-done.2
  47.9 5.5 %window.1 = f32[1,3,64,128]{3,2,1,0:T(8,128)} custom-call(s32[64]{0:T(128)S(1)} %get-tuple-element.8.place_ref, s32[64]{0:T(128)S(1)} %get-tuple-element.9.host_ref, f32[1,3,64,128]{3,2,1,0:T(8,128)S(1)} %copy-done, f32[1,2,64,128]{3,2,1,0:T(8,128)S(1)} %copy-done.1, s32[1,2,64,128]{3,2,1,0:T(8,128)S(1)} %copy-done.2, f32[1536,128]{1,0:T(8,128)S(1)} %bitcast.5), custom_call_target="tpu_custom_call" | custom-call | tf_op jit(solution)/shard_map/window/pallas_call | solution.py:483
Async XLA Ops:
  22.9 1.5 %collective-permute-start = (f32[64,8,128]{2,1,0:T(8,128)S(1)}, f32[64,8,128]{2,1,0:T(8,128)S(1)}, u32[]{:S(2)}, u32[]{:S(2)}) collective-permute-start(f32[64,8,128]{2,1,0:T(8,128)S(1)} %all_to_all.10), channel_id=1, source_target_pairs={{0,64},{64,0},{1,65},{65,1},{2,66},{66,2},{3,67},{67,3},{4,68},{68... | collective-permute-start | bytes 786440 | tf_op jit(solution)/shard_map/ppermute | solution.py:470
  25.6 22.3 %copy-start = (f32[1,3,64,128]{3,2,1,0:T(8,128)S(1)}, f32[1,3,64,128]{3,2,1,0:T(8,128)}, u32[]{:S(2)}) copy-start(f32[1,3,64,128]{3,2,1,0:T(8,128)} %state_ref.1) | copy-start | bytes 294916
  25.6 22.3 %copy-start.1 = (f32[1,2,64,128]{3,2,1,0:T(8,128)S(1)}, f32[1,2,64,128]{3,2,1,0:T(8,128)}, u32[]{:S(2)}) copy-start(f32[1,2,64,128]{3,2,1,0:T(8,128)} %depth_ref.1) | copy-start | bytes 196612
  25.6 22.3 %copy-start.2 = (s32[1,2,64,128]{3,2,1,0:T(8,128)S(1)}, s32[1,2,64,128]{3,2,1,0:T(8,128)}, u32[]{:S(2)}) copy-start(s32[1,2,64,128]{3,2,1,0:T(8,128)} %open_ref.1) | copy-start | bytes 196612

commit v2 on v1

v2 whole, which is shorter than its diff:
```python
import functools

import jax
import jax.numpy as jnp
from jax import lax
from jax.experimental import pallas as pl
from jax.experimental.pallas import tpu as pltpu
from jax.sharding import PartitionSpec as P

PH = 8
PW = 32
RR = 4
K = 2
STEPS = 4
NESTS = 64
COURANT = 0.3

ROWS = 64
COLS = 128
FR = RR * PH
SPOTS = RR - 1
PEERS = 64
HALO = 4
EXT = ROWS + 2 * HALO
TOP = (RR - 1) * PH // 2
LEFT = PW // 2
CHAN = 7
UNIT = 4
TILE_BLOCK = UNIT * K * SPOTS
SLOT_BLOCK = UNIT * K * 2
HALF = COLS // 2
LAST = CHAN - 1
PART = LAST // 2

VMEM = pl.BlockSpec(memory_space=pltpu.VMEM)
SMEM = pl.BlockSpec(memory_space=pltpu.SMEM)


def div6(p):
    return (p * 10923) >> 16


def div3(p):
    return (p * 21846) >> 16


def pack_kernel(
    place_in, host_in, state_in, depth_in, open_in,
    out_ref, place_ref, host_ref, state_ref, depth_ref, open_ref, sems,
):
    moves = [
        pltpu.make_async_copy(source, target, sems.at[i])
        for i, (source, target) in enumerate(
            (
                (state_in, state_ref), (depth_in, depth_ref), (open_in, open_ref),
                (place_in, place_ref), (host_in, host_ref),
            )
        )
    ]
    for move in moves:
        move.start()
    for move in moves:
        move.wait()

    def channel(k, rows):
        if k < 3:
            return state_ref[0, k, rows, :]
        if k < 5:
            return depth_ref[0, k - 3, rows, :]
        return open_ref[0, k - 5, rows, :].astype(jnp.float32)

    first = lax.broadcasted_iota(jnp.int32, (8, COLS), 0) < HALO
    rims = [
        jnp.where(first, channel(k, pl.ds(0, 8)), channel(k, pl.ds(ROWS - 8, 8)))
        for k in range(CHAN)
    ]
    rims = jnp.concatenate(rims + [jnp.zeros((8, COLS), jnp.float32)], axis=0)
    left = lax.broadcasted_iota(jnp.int32, (FR, COLS), 1) < HALF
    for b in range(K):
        rows = pl.ds(b * FR, FR)
        for g in range(2):
            base = g * FR * 8 + b * UNIT
            for c in range(PART):
                out_ref[pl.ds(base + c, FR, stride=8), :] = channel(PART * g + c, rows)
            half = channel(LAST, rows)
            rim = rims[g * FR : (g + 1) * FR]
            if g == 1:
                half = pltpu.roll(half, HALF, 1)
            if b == 0:
                rim = pltpu.roll(rim, HALF, 1)
            out_ref[pl.ds(base + PART, FR, stride=8), :] = jnp.where(left, half, rim)


def clear_table(table_ref, first, count):
    for i in range(count):
        table_ref[first + i] = -1


def compact_tiles_kernel(place_ref, host_ref, own_ref, other_ref, out_ref):
    me = lax.axis_index("row") * lax.axis_size("nest") + lax.axis_index("nest")
    sub = lax.broadcasted_iota(jnp.int32, (8, COLS), 0)
    sub_lane = lax.broadcasted_iota(jnp.int32, (8, COLS), 1)
    used = (sub_lane < HALF) | ((sub & (UNIT - 1)) < PART)
    half_of = jnp.where(used, jnp.where(sub < UNIT, 0, 1), 2)

    out_ref[...] = jnp.zeros_like(out_ref)

    def place_one(n, carry):
        p = place_ref[n]
        h = host_ref[n]
        t = div6(p)
        u = p - 6 * t
        piece = other_ref[pl.ds(pl.multiple_of((h >> 1) * 8, 8), 8), :]
        piece = jnp.where((h & 1) != (u & 1), pltpu.roll(piece, UNIT, 0), piece)
        spot = pl.ds(pl.multiple_of(t * TILE_BLOCK + (u >> 1) * 8, 8), 8)
        pltpu.store(out_ref.at[spot, :], piece, mask=half_of == (u & 1))
        return carry

    lax.fori_loop(0, NESTS, place_one, 0, unroll=8)

    tile = lax.broadcasted_iota(jnp.int32, (PEERS, COLS), 0)
    lane = lax.broadcasted_iota(jnp.int32, (PEERS, COLS), 1)
    tile_col = tile & 7
    has_right, has_left = tile_col < 7, tile_col > 0
    lower_half = me < FR
    to_above = ((me >> 2) & 1) == 0

    def right_of(x):
        return pltpu.roll(x, PEERS - 1, 0)

    def left_of(x):
        return pltpu.roll(x, 1, 0)

    def row_of(i):
        return own_ref[pl.ds(i, PEERS, stride=8), :]

    packed = jnp.zeros((PEERS, COLS), jnp.float32)
    rims = []
    for b in range(K):
        for c in range(PART):
            x = row_of(UNIT * b + c)
            side = jnp.where(
                has_right & (lane < HALO),
                right_of(x),
                jnp.where(has_left & (lane >= COLS - HALO), left_of(x), 0.0),
            )
            packed += pltpu.roll(side, HALF + HALO + 8 * (PART * b + c), 1)
        x = row_of(UNIT * b + PART)
        right = jnp.where(has_right & (lane < HALO), right_of(x), 0.0)
        left = jnp.where(has_left & (lane >= HALF - HALO) & (lane < HALF), left_of(x), 0.0)
        spot = HALF + 8 * PART * K + HALO * b
        packed += jnp.where(
            lower_half, pltpu.roll(right, spot, 1), pltpu.roll(left, spot - HALF + HALO, 1)
        )
        rims.append(
            jnp.where(
                to_above,
                jnp.where(tile < PEERS - 8, pltpu.roll(x, PEERS - 8, 0), 0.0),
                jnp.where(tile >= 8, pltpu.roll(x, 8, 0), 0.0),
            )
        )
    right = jnp.where(has_right & (lane >= HALF) & (lane < HALF + HALO), right_of(rims[0]), 0.0)
    left = jnp.where(has_left & (lane >= COLS - HALO), left_of(rims[1]), 0.0)
    packed += pltpu.roll(right, HALF - HALO, 1) + pltpu.roll(left, COLS - HALO, 1)
    for u, value in enumerate([packed] + rims):
        spot = pl.ds(UNIT * u + PART, PEERS, stride=TILE_BLOCK)
        out_ref[spot, :] = jnp.where(lane >= HALF, value, out_ref[spot, :])


def compact_slots_kernel(place_ref, host_ref, own_ref, other_ref, out_ref, table_ref):
    me = lax.axis_index("row") * lax.axis_size("nest") + lax.axis_index("nest")
    sub = lax.broadcasted_iota(jnp.int32, (UNIT, COLS), 0)
    lane = lax.broadcasted_iota(jnp.int32, (UNIT, COLS), 1)
    from_east = jnp.where(sub < PART, (lane < HALF).astype(jnp.int32), (me < FR).astype(jnp.int32))

    def unit(source_ref, i):
        piece = source_ref[pl.ds(pl.multiple_of((i >> 1) * 8, 8), 8), :]
        return jnp.where((i & 1) == 1, piece[UNIT:], piece[:UNIT])

    def clear(n, carry):
        clear_table(table_ref, 3 * div3(place_ref[n]), SPOTS)
        return carry

    def note(n, carry):
        table_ref[place_ref[n]] = host_ref[n]
        return carry

    def gather_band(n, carry):
        p = place_ref[n]
        h = host_ref[n]
        band = div3(p)
        j = p - 3 * band
        west = table_ref[3 * band + jnp.where(j == 0, 0, j - 1)]
        east = table_ref[3 * band + jnp.where(j == SPOTS - 1, SPOTS - 1, j + 1)]
        west = jnp.where(west < 0, 0, west)
        east = jnp.where(east < 0, 0, east)
        beside = jnp.where(from_east == 1, unit(own_ref, east), unit(own_ref, west))
        block = jnp.concatenate([unit(other_ref, band), beside], axis=0)
        out_ref[pl.ds(pl.multiple_of(h * 8, 8), 8), :] = block
        return carry

    out_ref[...] = jnp.zeros_like(out_ref)
    lax.fori_loop(0, NESTS, clear, 0, unroll=8)
    lax.fori_loop(0, NESTS, note, 0, unroll=8)
    lax.fori_loop(0, NESTS, gather_band, 0, unroll=4)


def window_kernel(
    tile_side, place_ref, host_ref, state_ref, depth_ref, open_ref, got_ref, out_ref,
    outer_ref, fine_ref, rep_ref, table_ref,
):
    row = lax.axis_index("row")
    col = lax.axis_index("nest")
    row_count = lax.axis_size("row")
    col_count = lax.axis_size("nest")
    me = row * col_count + col
    block = TILE_BLOCK if tile_side else SLOT_BLOCK
    lane = lax.broadcasted_iota(jnp.int32, (FR, COLS), 1)
    fine_row = lax.broadcasted_iota(jnp.int32, (FR, COLS), 0)
    small_lane = lax.broadcasted_iota(jnp.int32, (PH, COLS), 1)

    def own(k, rows):
        if k < 3:
            return state_ref[0, k, rows, :]
        if k < 5:
            return depth_ref[0, k - 3, rows, :]
        return open_ref[0, k - 5, rows, :].astype(jnp.float32)

    def rows_of(peer, row, count):
        return got_ref[pl.ds(peer * block + row, count, stride=block), :]

    def got(k, unit):
        if k < LAST:
            return rows_of((k // PART) * FR, UNIT * unit + k % PART, FR)
        left, right = (rows_of(g * FR, UNIT * unit + PART, FR) for g in range(2))
        return jnp.where(lane < HALF, left, pltpu.roll(right, HALF, 1))

    def set_fine(nest, values):
        level, east_flux, south_flux, depth_east, depth_south, open_east, open_south = values
        fine_ref[nest, 0] = level
        fine_ref[nest, 1] = COURANT * east_flux
        fine_ref[nest, 2] = COURANT * south_flux
        fine_ref[nest, 3] = (COURANT * COURANT) * open_east * depth_east
        fine_ref[nest, 4] = (COURANT * COURANT) * open_south * depth_south
        fine_ref[nest, 5] = open_east
        fine_ref[nest, 6] = open_south

    def note_place(n, carry):
        table_ref[place_ref[n]] = 1
        return carry

    def note_host(n, carry):
        table_ref[host_ref[n]] = place_ref[n]
        return carry

    if tile_side:
        clear_table(table_ref, 6 * me, K * SPOTS)
        lax.fori_loop(0, NESTS, note_place, 0, unroll=16)
        covered = [table_ref[6 * me + u] == 1 for u in range(K * SPOTS)]
        keep = (lane < HALO) | (lane >= COLS - HALO)
        small_keep = (small_lane < HALO) | (small_lane >= COLS - HALO)
        beside = [rows_of(g * FR, PART, FR) for g in range(2)]
        for k in range(CHAN):
            for b in range(K):
                rows = pl.ds(HALO + b * FR, FR)
                outer_ref[k, rows, 0:COLS] = own(k, pl.ds(b * FR, FR))
                if k < LAST:
                    shift = HALF + HALO + 8 * (PART * b + k % PART)
                    side = pltpu.roll(beside[k // PART], COLS - shift, 1)
                else:
                    shift = HALF + 8 * PART * K + HALO * b
                    side = jnp.where(
                        lane < HALO,
                        pltpu.roll(beside[0], COLS - shift, 1),
                        pltpu.roll(beside[1], COLS - HALO - shift, 1),
                    )
                outer_ref[k, rows, COLS : 2 * COLS] = jnp.where(keep, side, 0.0)
            rim = jnp.where(
                small_lane < HALF,
                pltpu.roll(rows_of(8 * k, UNIT + PART, 8), HALF, 1),
                rows_of(8 * k, 2 * UNIT + PART, 8),
            )
            corner = jnp.where(small_keep, pltpu.roll(rows_of(8 * k, PART, 8), HALO, 1), 0.0)
            for columns, value in ((pl.ds(0, COLS), rim), (pl.ds(COLS, COLS), corner)):
                outer_ref[k, EXT - HALO : EXT, columns] = value[:HALO]
                outer_ref[k, 0:HALO, columns] = value[HALO:]
        for u in range(K * SPOTS):
            set_fine(u, [got(k, u) for k in range(CHAN)])
    else:
        clear_table(table_ref, K * me, K)
        lax.fori_loop(0, NESTS, note_host, 0, unroll=16)
        at = [table_ref[K * me + s] for s in range(K)]
        live = [p >= 0 for p in at]
        bands = [3 * div3(jnp.where(live[s], at[s], 0)) for s in range(K)]
        spots = [jnp.where(live[s], at[s] - bands[s], 0) for s in range(K)]
        for s in range(K):
            clear_table(table_ref, bands[s], SPOTS)
        lax.fori_loop(0, NESTS, note_place, 0, unroll=16)
        covered = [table_ref[bands[s] + j] == 1 for s in range(K) for j in range(SPOTS)]
        for s in range(K):
            beside = [got(k, 2 * s + 1) for k in range(CHAN)]
            for j in range(SPOTS):
                set_fine(SPOTS * s + j, beside)
            set_fine(SPOTS * s + spots[s], [own(k, pl.ds(s * FR, FR)) for k in range(CHAN)])
            for k in range(CHAN):
                outer_ref[k, pl.ds(HALO + s * FR, FR), 0:COLS] = got(k, 2 * s)
        for k in range(CHAN):
            outer_ref[k, 0:HALO, 0:COLS] = jnp.zeros((HALO, COLS), jnp.float32)
            outer_ref[k, EXT - HALO : EXT, 0:COLS] = jnp.zeros((HALO, COLS), jnp.float32)
            outer_ref[k, :, COLS : 2 * COLS] = jnp.zeros((EXT, COLS), jnp.float32)

    for flux in (1, 2):
        outer_ref[flux] = COURANT * outer_ref[flux]
        outer_ref[flux + 2] = (COURANT * COURANT) * outer_ref[flux + 4] * outer_ref[flux + 2]

    inside = None
    if tile_side:
        ext_row = lax.broadcasted_iota(jnp.int32, (EXT, 2 * COLS), 0)
        ext_lane = lax.broadcasted_iota(jnp.int32, (EXT, 2 * COLS), 1)
        row_low = jnp.where(row == 0, HALO, 0)
        row_high = jnp.where(row == row_count - 1, EXT - HALO, EXT)
        right_end = jnp.where(col < col_count - 1, COLS + HALO, COLS)
        left_start = jnp.where(col > 0, 2 * COLS - HALO, 2 * COLS)
        inside = (
            (ext_row >= row_low)
            & (ext_row < row_high)
            & ((ext_lane < right_end) | (ext_lane >= left_start))
        )

    spread = [LEFT + PW * j + (small_lane >> 2) for j in range(SPOTS)]
    gathered = [
        jnp.clip(RR * (small_lane - LEFT - PW * j), 0, COLS - RR) for j in range(SPOTS)
    ]
    mine = [
        (small_lane >= LEFT + PW * j) & (small_lane < LEFT + PW * (j + 1)) for j in range(SPOTS)
    ]
    half_square = 0.5 * COURANT * COURANT

    def take(x, index):
        return jnp.take_along_axis(x, index, axis=1, mode="promise_in_bounds")

    def ghosts(surface, eastward, southward, slot):
        ends = []
        for b in range(K):
            r0 = HALO + TOP + b * FR
            e_rows = eastward[r0 : r0 + PH, :COLS]
            s_rows = surface[r0 : r0 + PH, :COLS]
            north = jnp.broadcast_to(southward[r0 - 1 : r0, :COLS], (PH, COLS))
            south = jnp.broadcast_to(surface[r0 + PH : r0 + PH + 1, :COLS], (PH, COLS))
            for j in range(SPOTS):
                c0 = LEFT + PW * j
                west = pltpu.roll(e_rows, COLS - (c0 - 1), 1)
                east = pltpu.roll(s_rows, COLS - 1 - (c0 + PW), 1)
                side = jnp.where(small_lane == 0, west, east)
                for i in range(RR):
                    rep_ref[slot, 3 * b + j, pl.ds(i, PH, stride=RR), :] = side
                ends.append((take(north, spread[j]), take(south, spread[j])))
        return ends

    def tall(x):
        return jnp.concatenate([x] * RR, axis=0)

    old_ends = ghosts(outer_ref[0], outer_ref[1], outer_ref[2], 0)
    for step in range(STEPS):
        old, new = step % 2, (step + 1) % 2
        surface, eastward, southward = outer_ref[0], outer_ref[1], outer_ref[2]
        flow = (eastward - pltpu.roll(eastward, 1, 1)) + (southward - pltpu.roll(southward, 1, 0))
        surface = surface - flow
        if inside is not None:
            surface = jnp.where(inside, surface, 0.0)
        to_east = pltpu.roll(surface, 2 * COLS - 1, 1)
        to_south = pltpu.roll(surface, EXT - 1, 0)
        eastward = outer_ref[5] * (
            eastward - half_square * (surface + to_east) * (to_east - surface)
        ) - outer_ref[3] * (to_east - surface)
        southward = outer_ref[6] * (
            southward - half_square * (surface + to_south) * (to_south - surface)
        ) - outer_ref[4] * (to_south - surface)
        outer_ref[0] = surface
        outer_ref[1] = eastward
        outer_ref[2] = southward
        new_ends = ghosts(surface, eastward, southward, new)
        for nest in range(K * SPOTS):
            b, j = nest // SPOTS, nest % SPOTS
            level, east_flux, south_flux = (fine_ref[nest, k] for k in range(3))
            old_side, new_side = rep_ref[old, nest], rep_ref[new, nest]
            (old_north, old_south), (new_north, new_south) = old_ends[nest], new_ends[nest]
            for m in range(1, RR + 1):
                part = m / RR
                side = old_side + part * (new_side - old_side)
                north = tall(old_north + part * (new_north - old_north))
                south = tall(old_south + part * (new_south - old_south))
                west_of = jnp.where(lane == 0, side, pltpu.roll(east_flux, 1, 1))
                north_of = jnp.where(fine_row == 0, north, pltpu.roll(south_flux, 1, 0))
                level = level - ((east_flux - west_of) + (south_flux - north_of))
                east_of = jnp.where(lane == COLS - 1, side, pltpu.roll(level, COLS - 1, 1))
                south_of = jnp.where(fine_row == FR - 1, south, pltpu.roll(level, FR - 1, 0))
                open_east, open_south = fine_ref[nest, 5], fine_ref[nest, 6]
                if step == 0 and m == 1:
                    east_flux = open_east * east_flux
                    south_flux = open_south * south_flux
                east_flux = east_flux - (
                    fine_ref[nest, 3] + (half_square * open_east) * (level + east_of)
                ) * (east_of - level)
                south_flux = south_flux - (
                    fine_ref[nest, 4] + (half_square * open_south) * (level + south_of)
                ) * (south_of - level)
            for k, value in enumerate((level, east_flux, south_flux)):
                fine_ref[nest, k] = value

            def every(k, i):
                return fine_ref[nest, k, pl.ds(i, PH, stride=RR), :]

            def quads(x):
                x = x + pltpu.roll(x, COLS - 1, 1)
                return x + pltpu.roll(x, COLS - 2, 1)

            mean_level = quads((every(0, 0) + every(0, 1)) + (every(0, 2) + every(0, 3)))
            mean_east = (every(1, 0) + every(1, 1)) + (every(1, 2) + every(1, 3))
            mean_south = quads(every(2, RR - 1))
            back = (
                take(mean_level, gathered[j]) * (1.0 / (RR * RR)),
                take(mean_east, gathered[j] + (RR - 1)) * (1.0 / RR),
                take(mean_south, gathered[j]) * (1.0 / RR),
            )
            here = mine[j] & covered[nest]
            rows = pl.ds(HALO + TOP + b * FR, PH)
            for k in range(3):
                outer_ref[k, rows, 0:COLS] = jnp.where(here, back[k], outer_ref[k, rows, 0:COLS])
        old_ends = new_ends

    for k in range(3):
        scale = 1.0 if k == 0 else 1.0 / COURANT
        if tile_side:
            out_ref[0, k] = outer_ref[k, HALO : HALO + ROWS, 0:COLS] * scale
        else:
            for s in range(K):
                rows = pl.ds(s * FR, FR)
                out_ref[0, k, rows, :] = jnp.where(
                    live[s], fine_ref[SPOTS * s + spots[s], k] * scale, state_ref[0, k, rows, :]
                )


def window(tile_side, place, host, pieces, others, state, depth, opening):
    block = TILE_BLOCK if tile_side else SLOT_BLOCK
    table = pltpu.SMEM((PEERS * K * SPOTS,), jnp.int32)
    blocks = pl.pallas_call(
        compact_tiles_kernel if tile_side else compact_slots_kernel,
        out_shape=jax.ShapeDtypeStruct((PEERS * block, COLS), jnp.float32),
        in_specs=[SMEM, SMEM, VMEM, VMEM],
        out_specs=VMEM,
        scratch_shapes=[] if tile_side else [table],
        compiler_params=pltpu.CompilerParams(vmem_limit_bytes=8 * 1024 * 1024),
        name="compact_tiles" if tile_side else "compact_slots",
    )(place, host, pieces.reshape(-1, COLS), others.reshape(-1, COLS))
    got = lax.all_to_all(
        blocks.reshape(PEERS, block, COLS),
        ("row", "nest"),
        split_axis=0,
        concat_axis=0,
        tiled=True,
    )
    return pl.pallas_call(
        functools.partial(window_kernel, tile_side),
        out_shape=jax.ShapeDtypeStruct(state.shape, jnp.float32),
        in_specs=[SMEM, SMEM, VMEM, VMEM, VMEM, VMEM],
        out_specs=VMEM,
        scratch_shapes=[
            pltpu.VMEM((CHAN, EXT, 2 * COLS), jnp.float32),
            pltpu.VMEM((K * SPOTS, CHAN, FR, COLS), jnp.float32),
            pltpu.VMEM((2, K * SPOTS, FR, COLS), jnp.float32),
            table,
        ],
        compiler_params=pltpu.CompilerParams(vmem_limit_bytes=32 * 1024 * 1024),
        name="window_tiles" if tile_side else "window_slots",
    )(place, host, state, depth, opening, got.reshape(-1, COLS))


def on_device(ocean_state, face_depth, face_open, nest_place, nest_host):
    tiles = ("row", "nest")
    packed, place, host = pl.pallas_call(
        pack_kernel,
        out_shape=(
            jax.ShapeDtypeStruct((PEERS * 8, COLS), jnp.float32),
            jax.ShapeDtypeStruct(nest_place.shape, jnp.int32),
            jax.ShapeDtypeStruct(nest_host.shape, jnp.int32),
        ),
        in_specs=[pl.BlockSpec(memory_space=pltpu.HBM)] * 5,
        out_specs=(VMEM, VMEM, VMEM),
        scratch_shapes=[
            pltpu.VMEM(ocean_state.shape, jnp.float32),
            pltpu.VMEM(face_depth.shape, jnp.float32),
            pltpu.VMEM(face_open.shape, jnp.int32),
            pltpu.SemaphoreType.DMA((5,)),
        ],
        compiler_params=pltpu.CompilerParams(vmem_limit_bytes=4 * 1024 * 1024),
        name="pack",
    )(*(
        pltpu.with_memory_space_constraint(x, pltpu.HBM)
        for x in (nest_place, nest_host, ocean_state, face_depth, face_open)
    ))
    pieces = lax.all_to_all(
        packed.reshape(PEERS, 8, COLS), tiles, split_axis=0, concat_axis=0, tiled=True
    )
    others = lax.ppermute(pieces, "sec", [(0, 1), (1, 0)])
    return lax.cond(
        lax.axis_index("sec") == 0,
        functools.partial(window, True),
        functools.partial(window, False),
        place, host, pieces, others, ocean_state, face_depth, face_open,
    )


def solution(mesh):
    placed = (
        P("sec", None, "row", "nest"),
        P("sec", None, "row", "nest"),
        P("sec", None, "row", "nest"),
        P(),
        P(),
    )
    return jax.shard_map(
        on_device,
        mesh=mesh,
        in_specs=placed,
        out_specs=P("sec", None, "row", "nest"),
        check_vma=False,
    )
```

time: 54.5 us -> 51.4 us (0.943); the launches traced: 53.5 us -> 51.2 us
  blocking collectives: 44.1 us -> 42.2 us
  Pallas kernels: 7.79 us -> 6.77 us
  local copies, waits for them, and re-layouts: 0.02 us -> 0.66 us
    all_to_all x1, blocking collectives: 22.3 us -> 20.2 us  [window(): lax.all_to_all(blocks.reshape(PEERS, block, COLS), ('row', 'nest'), split...]
    pallas_call x2, Pallas kernels: 6.72 us -> 5.69 us  [the longest x1 4.53 us: window(): pl.pallas_call(functools.partial(window_kernel, tile_side), out_shape=jax...]
    unnamed x6 -> x8, local copies, waits for them, and re-layouts: 0.02 us -> 0.66 us
where the time goes in v2:
time: 51.4 us; the launch traced here: 51.2 us
  blocking collectives  42.2 us (82%)
  Pallas kernels  6.77 us (13%)
  waiting for transfers between devices  1.53 us (3%)
  local copies, waits for them, and re-layouts  0.66 us (1%)
    all_to_all x1, blocking collectives, on_device(): lax.all_to_all(packed.reshape(PEERS, 8, COLS), tiles, split_axis=0, conca...  21.9 us
    all_to_all x1, blocking collectives, window(): lax.all_to_all(blocks.reshape(PEERS, block, COLS), ('row', 'nest'), split...  20.2 us
    pallas_call x1, Pallas kernels, window(): pl.pallas_call(functools.partial(window_kernel, tile_side), out_shape=jax...  4.53 us
    ppermute x1, waiting for transfers between devices, on_device(): others = lax.ppermute(pieces, 'sec', [(0, 1), (1, 0)])  1.53 us
    pallas_call x1, Pallas kernels, window(): pl.pallas_call(compact_tiles_kernel if tile_side else compact_slots_kerne...  1.16 us
    pallas_call x1, Pallas kernels, on_device(): pl.pallas_call(pack_kernel, out_shape=(jax.ShapeDtypeStruct((PEERS * 8, C...  1.08 us
  transfers between devices with their start and end apart: 1, of which 1 were waited for; matrix products, arithmetic and copies ran while one was open for 0% of the time, Pallas kernels for 0%

profile of v2, /device:TPU:0, one launch (start us, length us, event | category | flops | bytes accessed | tf_op | source)
XLA Modules:
  0.0 51.2 jit_solution(1075932280347349379)
XLA Ops:
  0.0 1.1 %pack.1 = (f32[512,128]{1,0:T(8,128)S(1)}, s32[64]{0:T(128)S(1)}, s32[64]{0:T(128)S(1)}) custom-call(s32[64]{0:T(128)} %place_in.1, s32[64]{0:T(128)} %host_in.1, f32[1,3,64,128]{3,2,1,0:T(8,128)} %state_in.1, f32[1,2,64,128]{3,2,1,0:T(8,128)} %depth_in.1, s32[1,2,64,128]{3,2,1,0:T(8,128)} %open_in.1), custom_call_target="tpu_custom_call" | custom-call | tf_op jit(solution)/shard_map/pack/pallas_call | solution.py:481
  1.1 0.0 copy-start
  1.1 0.0 copy-start.1
  1.1 0.0 copy-start.2
  1.1 21.9 %all_to_all.15 = f32[64,8,128]{2,1,0:T(8,128)S(1)} all-to-all(f32[64,8,128]{2,1,0:T(8,128)S(1)} %bitcast.13), channel_id=1, replica_groups=mesh['sec'=2,'row'=8,'nest'=8] {'row','nest'}, dimensions={0} | all-to-all | bytes 524288 | tf_op jit(solution)/shard_map/all_to_all | solution.py:502
  23.1 0.0 collective-permute-start
  23.1 1.5 %collective-permute-done = f32[64,8,128]{2,1,0:T(8,128)S(1)} collective-permute-done((f32[64,8,128]{2,1,0:T(8,128)S(1)}, f32[64,8,128]{2,1,0:T(8,128)S(1)}, u32[]{:S(2)}, u32[]{:S(2)}) %collective-permute-start) | collective-permute-done | bytes 262176 | tf_op jit(solution)/shard_map/ppermute | solution.py:505
  24.6 0.0 copy-done
  24.6 0.0 copy-done.1
  24.6 0.0 copy-done.2
  24.6 25.9 %conditional.1 = (f32[1,3,64,128]{3,2,1,0:T(8,128)S(1)}) conditional(s32[]{:T(128)} %convert_element_type.3, (f32[64,8,128]{2,1,0:T(8,128)S(1)}, f32[64,8,128]{2,1,0:T(8,128)S(1)}, s32[64]{0:T(128)S(1)}, s32[64]{0:T(128)S(1)}, f32[1,3,64,128]{3,2,1,0:T(8,128)S(1)}, /*index=5*/f32[1,2,64,128]{3,2,1,0:T(8,128)S(1)}, ...), branch_computations={%region_0.0_spmd, %region_1.0_spmd} | conditional | bytes 1572872 | solution.py:506
  24.6 1.2 %compact_tiles.1 = f32[1536,128]{1,0:T(8,128)S(1)} custom-call(s32[64]{0:T(128)S(1)} %get-tuple-element.43.place_ref, s32[64]{0:T(128)S(1)} %get-tuple-element.44.host_ref, f32[512,128]{1,0:T(8,128)S(1)} %bitcast.15, f32[512,128]{1,0:T(8,128)S(1)} %bitcast.17), custom_call_target="tpu_custom_call" | custom-call | tf_op jit(solution)/shard_map/cond/branch_1_fun/compact_tiles/pallas_call | solution.py:447
  25.8 20.2 %all_to_all.14 = f32[64,24,128]{2,1,0:T(8,128)S(1)} all-to-all(f32[64,24,128]{2,1,0:T(8,128)S(1)} %bitcast.10), channel_id=1, replica_groups=mesh['sec'=2,'row'=8,'nest'=8] {'row','nest'}, dimensions={0} | all-to-all | bytes 1572864 | tf_op jit(solution)/shard_map/cond/branch_1_fun/all_to_all | solution.py:456
  46.0 4.5 %window_tiles.1 = f32[1,3,64,128]{3,2,1,0:T(8,128)S(1)} custom-call(s32[64]{0:T(128)S(1)} %get-tuple-element.43.place_ref, s32[64]{0:T(128)S(1)} %get-tuple-element.44.host_ref, f32[1,3,64,128]{3,2,1,0:T(8,128)S(1)} %get-tuple-element.45.state_ref, f32[1,2,64,128]{3,2,1,0:T(8,128)S(1)} %get-tuple-element.46.depth_ref, ...), custom_call_target="tpu_custom_call" | custom-call | tf_op jit(solution)/shard_map/cond/branch_1_fun/window_tiles/pallas_call | solution.py:463
  50.6 0.0 copy-start.3
  50.6 0.6 %copy-done.3 = f32[1,3,64,128]{3,2,1,0:T(8,128)} copy-done((f32[1,3,64,128]{3,2,1,0:T(8,128)}, f32[1,3,64,128]{3,2,1,0:T(8,128)S(1)}, u32[]{:S(2)}) %copy-start.3) | copy-done | bytes 98328
Async XLA Ops:
  1.1 23.5 %copy-start = (f32[1,3,64,128]{3,2,1,0:T(8,128)S(1)}, f32[1,3,64,128]{3,2,1,0:T(8,128)}, u32[]{:S(2)}) copy-start(f32[1,3,64,128]{3,2,1,0:T(8,128)} %state_in.1) | copy-start | bytes 294916
  1.1 23.5 %copy-start.1 = (f32[1,2,64,128]{3,2,1,0:T(8,128)S(1)}, f32[1,2,64,128]{3,2,1,0:T(8,128)}, u32[]{:S(2)}) copy-start(f32[1,2,64,128]{3,2,1,0:T(8,128)} %depth_in.1) | copy-start | bytes 196612
  1.1 23.5 %copy-start.2 = (s32[1,2,64,128]{3,2,1,0:T(8,128)S(1)}, s32[1,2,64,128]{3,2,1,0:T(8,128)}, u32[]{:S(2)}) copy-start(s32[1,2,64,128]{3,2,1,0:T(8,128)} %open_in.1) | copy-start | bytes 196612
  23.1 1.5 %collective-permute-start = (f32[64,8,128]{2,1,0:T(8,128)S(1)}, f32[64,8,128]{2,1,0:T(8,128)S(1)}, u32[]{:S(2)}, u32[]{:S(2)}) collective-permute-start(f32[64,8,128]{2,1,0:T(8,128)S(1)} %all_to_all.15), channel_id=1, source_target_pairs={{0,64},{64,0},{1,65},{65,1},{2,66},{66,2},{3,67},{67,3},{4,68},{68... | collective-permute-start | bytes 786440 | tf_op jit(solution)/shard_map/ppermute | solution.py:505
  50.6 0.6 %copy-start.3 = (f32[1,3,64,128]{3,2,1,0:T(8,128)}, f32[1,3,64,128]{3,2,1,0:T(8,128)S(1)}, u32[]{:S(2)}) copy-start(f32[1,3,64,128]{3,2,1,0:T(8,128)S(1)} %get-tuple-element.61) | copy-start | bytes 294916

commit v3 on v2

v3 whole, which is shorter than its diff:
```python
import functools
from typing import NamedTuple

import jax
import jax.numpy as jnp
from jax import lax
from jax.experimental import pallas as pl
from jax.experimental.pallas import tpu as pltpu
from jax.sharding import PartitionSpec as P

PH = 8
PW = 32
RR = 4
K = 2
STEPS = 4
NESTS = 64
COURANT = 0.3

ROWS = 64
COLS = 128
FR = RR * PH
SPOTS = RR - 1
PEERS = 64
HALO = 4
EXT = ROWS + 2 * HALO
TOP = (RR - 1) * PH // 2
LEFT = PW // 2
CHAN = 7
UNIT = 4
FEW = 4
MANY = K * SPOTS
SLOT_UNITS = K
HALF = COLS // 2
LAST = CHAN - 1
PART = LAST // 2
HALF_SQUARE = 0.5 * COURANT * COURANT

VMEM = pl.BlockSpec(memory_space=pltpu.VMEM)
SMEM = pl.BlockSpec(memory_space=pltpu.SMEM)


def div6(p):
    return (p * 10923) >> 16


def div3(p):
    return (p * 21846) >> 16


def pack_kernel(
    place_in, host_in, state_in, depth_in, open_in,
    out_ref, place_ref, host_ref, crowded_out,
    state_ref, depth_ref, open_ref, crowded_ref, sems,
):
    moves = [
        pltpu.make_async_copy(source, target, sems.at[i])
        for i, (source, target) in enumerate(
            (
                (place_in, place_ref), (host_in, host_ref),
                (state_in, state_ref), (depth_in, depth_ref), (open_in, open_ref),
            )
        )
    ]
    for move in moves:
        move.start()
    for move in moves[:2]:
        move.wait()
    tile = lax.broadcasted_iota(jnp.int32, (PEERS, NESTS), 0)
    hits = jnp.where(div6(place_ref[...]) == tile, 1.0, 0.0)
    most = jnp.max(jnp.sum(hits, axis=1, keepdims=True), axis=0, keepdims=True)
    crowded_ref[...] = jnp.where(most > FEW, 1, 0)
    report = pltpu.make_async_copy(crowded_ref, crowded_out, sems.at[len(moves)])
    report.start()
    for move in moves[2:]:
        move.wait()

    def channel(k, rows):
        if k < 3:
            return state_ref[0, k, rows, :]
        if k < 5:
            return depth_ref[0, k - 3, rows, :]
        return open_ref[0, k - 5, rows, :].astype(jnp.float32)

    first = lax.broadcasted_iota(jnp.int32, (8, COLS), 0) < HALO
    rims = [
        jnp.where(first, channel(k, pl.ds(0, 8)), channel(k, pl.ds(ROWS - 8, 8)))
        for k in range(CHAN)
    ]
    rims = jnp.concatenate(rims + [jnp.zeros((8, COLS), jnp.float32)], axis=0)
    left = lax.broadcasted_iota(jnp.int32, (FR, COLS), 1) < HALF
    for b in range(K):
        rows = pl.ds(b * FR, FR)
        for g in range(2):
            base = g * FR * 8 + b * UNIT
            for c in range(PART):
                out_ref[pl.ds(base + c, FR, stride=8), :] = channel(PART * g + c, rows)
            half = channel(LAST, rows)
            rim = rims[g * FR : (g + 1) * FR]
            if g == 1:
                half = pltpu.roll(half, HALF, 1)
            if b == 0:
                rim = pltpu.roll(rim, HALF, 1)
            out_ref[pl.ds(base + PART, FR, stride=8), :] = jnp.where(left, half, rim)
    report.wait()


def clear_table(table_ref, first, count, value=-1):
    for i in range(count):
        table_ref[first + i] = value


def compact_tiles_kernel(units, place_ref, host_ref, own_ref, other_ref, out_ref, table_ref):
    block = UNIT * units
    me = lax.axis_index("row") * lax.axis_size("nest") + lax.axis_index("nest")
    sub = lax.broadcasted_iota(jnp.int32, (8, COLS), 0)
    sub_lane = lax.broadcasted_iota(jnp.int32, (8, COLS), 1)
    used = (sub_lane < HALF) | ((sub & (UNIT - 1)) < PART)
    half_of = jnp.where(used, jnp.where(sub < UNIT, 0, 1), 2)

    out_ref[...] = jnp.zeros_like(out_ref)
    clear_table(table_ref, 0, PEERS, 0)

    def place_one(n, carry):
        h = host_ref[0, n]
        t = div6(place_ref[0, n])
        u = table_ref[t]
        table_ref[t] = u + 1
        piece = other_ref[pl.ds(pl.multiple_of((h >> 1) * 8, 8), 8), :]
        piece = jnp.where((h & 1) != (u & 1), pltpu.roll(piece, UNIT, 0), piece)
        spot = pl.ds(pl.multiple_of(t * block + (u >> 1) * 8, 8), 8)
        pltpu.store(out_ref.at[spot, :], piece, mask=half_of == (u & 1))
        return carry

    lax.fori_loop(0, NESTS, place_one, 0, unroll=8)

    tile = lax.broadcasted_iota(jnp.int32, (PEERS, COLS), 0)
    lane = lax.broadcasted_iota(jnp.int32, (PEERS, COLS), 1)
    tile_col = tile & 7
    has_right, has_left = tile_col < 7, tile_col > 0
    lower_half = me < FR
    to_above = ((me >> 2) & 1) == 0

    def right_of(x):
        return pltpu.roll(x, PEERS - 1, 0)

    def left_of(x):
        return pltpu.roll(x, 1, 0)

    def row_of(i):
        return own_ref[pl.ds(i, PEERS, stride=8), :]

    packed = jnp.zeros((PEERS, COLS), jnp.float32)
    rims = []
    for b in range(K):
        for c in range(PART):
            x = row_of(UNIT * b + c)
            side = jnp.where(
                has_right & (lane < HALO),
                right_of(x),
                jnp.where(has_left & (lane >= COLS - HALO), left_of(x), 0.0),
            )
            packed += pltpu.roll(side, HALF + HALO + 8 * (PART * b + c), 1)
        x = row_of(UNIT * b + PART)
        right = jnp.where(has_right & (lane < HALO), right_of(x), 0.0)
        left = jnp.where(has_left & (lane >= HALF - HALO) & (lane < HALF), left_of(x), 0.0)
        spot = HALF + 8 * PART * K + HALO * b
        packed += jnp.where(
            lower_half, pltpu.roll(right, spot, 1), pltpu.roll(left, spot - HALF + HALO, 1)
        )
        rims.append(
            jnp.where(
                to_above,
                jnp.where(tile < PEERS - 8, pltpu.roll(x, PEERS - 8, 0), 0.0),
                jnp.where(tile >= 8, pltpu.roll(x, 8, 0), 0.0),
            )
        )
    right = jnp.where(has_right & (lane >= HALF) & (lane < HALF + HALO), right_of(rims[0]), 0.0)
    left = jnp.where(has_left & (lane >= COLS - HALO), left_of(rims[1]), 0.0)
    packed += pltpu.roll(right, HALF - HALO, 1) + pltpu.roll(left, COLS - HALO, 1)
    for u, value in enumerate([packed] + rims):
        spot = pl.ds(UNIT * u + PART, PEERS, stride=block)
        out_ref[spot, :] = jnp.where(lane >= HALF, value, out_ref[spot, :])


def compact_slots_kernel(place_ref, host_ref, own_ref, other_ref, out_ref, table_ref):
    me = lax.axis_index("row") * lax.axis_size("nest") + lax.axis_index("nest")
    sub = lax.broadcasted_iota(jnp.int32, (8, COLS), 0)
    lane = lax.broadcasted_iota(jnp.int32, (8, COLS), 1)
    whole = (sub & (UNIT - 1)) < PART
    half_of = jnp.where(sub < UNIT, 0, 1)
    is_outer = jnp.where(whole, jnp.where((lane >= PW) & (lane < COLS - PW), 1, 0), 0)
    is_outer = jnp.where(whole | (lane < HALF), is_outer, 1)
    is_east = jnp.where(whole, jnp.where(lane < HALF, 1, 0), jnp.where(me < FR, 1, 0))

    def unit(source_ref, i):
        piece = source_ref[pl.ds(pl.multiple_of((i >> 1) * 8, 8), 8), :]
        return jnp.where(half_of == (i & 1), piece, pltpu.roll(piece, UNIT, 0))

    def clear(n, carry):
        clear_table(table_ref, 3 * div3(place_ref[0, n]), SPOTS, 0)
        return carry

    def note(n, carry):
        table_ref[place_ref[0, n]] = host_ref[0, n]
        return carry

    def gather_band(n, carry):
        p = place_ref[0, n]
        h = host_ref[0, n]
        band = div3(p)
        j = p - 3 * band
        west = unit(own_ref, table_ref[3 * band + jnp.where(j == 0, 0, j - 1)])
        east = unit(own_ref, table_ref[3 * band + jnp.where(j == SPOTS - 1, SPOTS - 1, j + 1)])
        outer = unit(other_ref, band)
        moved = jnp.where(
            j == 0, pltpu.roll(outer, PW, 1), jnp.where(j == 1, outer, pltpu.roll(outer, COLS - PW, 1))
        )
        outer = jnp.where(whole, moved, pltpu.roll(outer, HALF, 1))
        value = jnp.where(is_outer == 1, outer, jnp.where(is_east == 1, east, west))
        spot = pl.ds(pl.multiple_of((h >> 1) * 8, 8), 8)
        pltpu.store(out_ref.at[spot, :], value, mask=half_of == (h & 1))
        return carry

    out_ref[...] = jnp.zeros_like(out_ref)
    lax.fori_loop(0, NESTS, clear, 0, unroll=8)
    lax.fori_loop(0, NESTS, note, 0, unroll=8)
    lax.fori_loop(0, NESTS, gather_band, 0, unroll=4)


class Nest(NamedTuple):
    row: int | jax.Array
    west: jax.Array
    east: jax.Array
    spread: jax.Array
    gather: jax.Array
    covers: jax.Array


def window_kernel(
    tile_side, units, place_ref, host_ref, state_ref, depth_ref, open_ref, got_ref, out_ref,
    outer_ref, fine_ref, rep_ref, table_ref,
):
    row = lax.axis_index("row")
    col = lax.axis_index("nest")
    row_count = lax.axis_size("row")
    col_count = lax.axis_size("nest")
    me = row * col_count + col
    block = UNIT * units
    lane = lax.broadcasted_iota(jnp.int32, (FR, COLS), 1)
    small_row = lax.broadcasted_iota(jnp.int32, (PH, COLS), 0)
    small_lane = lax.broadcasted_iota(jnp.int32, (PH, COLS), 1)

    def own(k, rows):
        if k < 3:
            return state_ref[0, k, rows, :]
        if k < 5:
            return depth_ref[0, k - 3, rows, :]
        return open_ref[0, k - 5, rows, :].astype(jnp.float32)

    def rows_of(peer, row, count):
        return got_ref[pl.ds(peer * block + row, count, stride=block), :]

    def got(k, unit):
        if k < LAST:
            return rows_of((k // PART) * FR, UNIT * unit + k % PART, FR)
        left, right = (rows_of(g * FR, UNIT * unit + PART, FR) for g in range(2))
        return jnp.where(lane < HALF, left, pltpu.roll(right, HALF, 1))

    def set_fine(nest, values):
        level, east_flux, south_flux, depth_east, depth_south, open_east, open_south = values
        fine_ref[nest, 0] = level
        fine_ref[nest, 1] = COURANT * east_flux
        fine_ref[nest, 2] = COURANT * south_flux
        fine_ref[nest, 3] = (COURANT * COURANT) * open_east * depth_east
        fine_ref[nest, 4] = (COURANT * COURANT) * open_south * depth_south
        fine_ref[nest, 5] = HALF_SQUARE * open_east
        fine_ref[nest, 6] = HALF_SQUARE * open_south

    if tile_side:

        def find(n, count):
            p = place_ref[0, n]
            table_ref[count] = p - 6 * me
            return count + jnp.where(div6(p) == me, 1, 0)

        count = lax.fori_loop(0, NESTS, find, 0, unroll=16)
        nests = []
        for u in range(units):
            p = jnp.where(u < count, table_ref[u], 0)
            b = jnp.where(p >= SPOTS, 1, 0)
            c0 = LEFT + PW * (p - SPOTS * b)
            offset = small_lane - c0
            nests.append(
                Nest(
                    HALO + TOP + FR * b,
                    c0 - 1,
                    c0 + PW,
                    c0 + (small_lane >> 2),
                    jnp.clip(RR * offset, 0, COLS - RR),
                    (offset >= 0) & (offset < PW) & (u < count),
                )
            )
        keep = (lane < HALO) | (lane >= COLS - HALO)
        small_keep = (small_lane < HALO) | (small_lane >= COLS - HALO)
        beside = [rows_of(g * FR, PART, FR) for g in range(2)]
        for k in range(CHAN):
            for b in range(K):
                rows = pl.ds(HALO + b * FR, FR)
                outer_ref[k, rows, 0:COLS] = own(k, pl.ds(b * FR, FR))
                if k < LAST:
                    shift = HALF + HALO + 8 * (PART * b + k % PART)
                    side = pltpu.roll(beside[k // PART], COLS - shift, 1)
                else:
                    shift = HALF + 8 * PART * K + HALO * b
                    side = jnp.where(
                        lane < HALO,
                        pltpu.roll(beside[0], COLS - shift, 1),
                        pltpu.roll(beside[1], COLS - HALO - shift, 1),
                    )
                outer_ref[k, rows, COLS : 2 * COLS] = jnp.where(keep, side, 0.0)
            rim = jnp.where(
                small_lane < HALF,
                pltpu.roll(rows_of(8 * k, UNIT + PART, 8), HALF, 1),
                rows_of(8 * k, 2 * UNIT + PART, 8),
            )
            corner = jnp.where(small_keep, pltpu.roll(rows_of(8 * k, PART, 8), HALO, 1), 0.0)
            for columns, value in ((pl.ds(0, COLS), rim), (pl.ds(COLS, COLS), corner)):
                outer_ref[k, EXT - HALO : EXT, columns] = value[:HALO]
                outer_ref[k, 0:HALO, columns] = value[HALO:]
        for u in range(units):
            set_fine(u, [got(k, u) for k in range(CHAN)])
    else:

        def note_host(n, carry):
            table_ref[host_ref[0, n]] = place_ref[0, n]
            return carry

        def note_place(n, carry):
            table_ref[place_ref[0, n]] = 1
            return carry

        clear_table(table_ref, K * me, K)
        lax.fori_loop(0, NESTS, note_host, 0, unroll=16)
        at = [table_ref[K * me + s] for s in range(K)]
        live = [p >= 0 for p in at]
        bands = [3 * div3(jnp.where(live[s], at[s], 0)) for s in range(K)]
        spots = [jnp.where(live[s], at[s] - bands[s], 0) for s in range(K)]
        for s in range(K):
            clear_table(table_ref, bands[s], SPOTS)
        lax.fori_loop(0, NESTS, note_place, 0, unroll=16)
        nests = []
        for s in range(K):
            j = spots[s]
            r0 = HALO + TOP + FR * s
            c0 = LEFT + PW * j
            offset = small_lane - c0
            west = (j > 0) & (table_ref[bands[s] + jnp.where(j > 0, j - 1, 0)] == 1)
            last = SPOTS - 1
            east = (j < last) & (table_ref[bands[s] + jnp.where(j < last, j + 1, last)] == 1)
            nests.append(
                Nest(
                    r0,
                    c0 - 1,
                    c0 + PW,
                    c0 + (small_lane >> 2),
                    jnp.clip(RR * offset, 0, COLS - RR),
                    (offset >= 0) & (offset < PW) & live[s],
                )
            )
            around = c0 + jnp.where(small_lane < HALF, PW, -PW) + (small_lane >> 2)
            nests.append(
                Nest(
                    r0,
                    c0 + PW - 1,
                    c0,
                    jnp.clip(around, 0, COLS - 1),
                    jnp.clip(RR * jnp.where(offset < 0, offset + PW, offset - PW), 0, COLS - RR),
                    ((offset >= -PH) & (offset < 0) & west)
                    | ((offset >= PW) & (offset < PW + PH) & east),
                )
            )
            set_fine(2 * s, [own(k, pl.ds(s * FR, FR)) for k in range(CHAN)])
            ends = [got(k, s) for k in range(CHAN)]
            set_fine(2 * s + 1, ends)
            for k in range(LAST):
                outer_ref[k, pl.ds(HALO + s * FR, FR), 0:COLS] = jnp.where(
                    j == 0,
                    pltpu.roll(ends[k], COLS - PW, 1),
                    jnp.where(j == 1, ends[k], pltpu.roll(ends[k], PW, 1)),
                )
            left, right = (rows_of(g * FR, UNIT * s + PART, FR) for g in range(2))
            outer_ref[LAST, pl.ds(HALO + s * FR, FR), 0:COLS] = jnp.where(
                lane < HALF, pltpu.roll(left, HALF, 1), right
            )
        for k in range(CHAN):
            outer_ref[k, 0:HALO, 0:COLS] = jnp.zeros((HALO, COLS), jnp.float32)
            outer_ref[k, EXT - HALO : EXT, 0:COLS] = jnp.zeros((HALO, COLS), jnp.float32)
            outer_ref[k, :, COLS : 2 * COLS] = jnp.zeros((EXT, COLS), jnp.float32)

    for flux in (1, 2):
        outer_ref[flux] = COURANT * outer_ref[flux]
        outer_ref[flux + 2] = (COURANT * COURANT) * outer_ref[flux + 4] * outer_ref[flux + 2]

    inside = None
    if tile_side:
        ext_row = lax.broadcasted_iota(jnp.int32, (EXT, 2 * COLS), 0)
        ext_lane = lax.broadcasted_iota(jnp.int32, (EXT, 2 * COLS), 1)
        row_low = jnp.where(row == 0, HALO, 0)
        row_high = jnp.where(row == row_count - 1, EXT - HALO, EXT)
        right_end = jnp.where(col < col_count - 1, COLS + HALO, COLS)
        left_start = jnp.where(col > 0, 2 * COLS - HALO, 2 * COLS)
        inside = (
            (ext_row >= row_low)
            & (ext_row < row_high)
            & ((ext_lane < right_end) | (ext_lane >= left_start))
        )


    def take(x, index):
        return jnp.take_along_axis(x, index, axis=1, mode="promise_in_bounds")

    def block_of(k, start):
        return outer_ref[k, pl.ds(pl.multiple_of(start, 8), PH), 0:COLS]

    def ghosts(slot):
        ends = []
        for i, nest in enumerate(nests):
            west = pltpu.roll(block_of(1, nest.row), COLS - nest.west, 1)
            east = pltpu.roll(block_of(0, nest.row), COLS - 1 - nest.east, 1)
            side = jnp.where(small_lane == 0, west, east)
            for m in range(RR):
                rep_ref[slot, i, pl.ds(m, PH, stride=RR), :] = side
            north = block_of(2, nest.row - PH)[PH - 1 :]
            south = block_of(0, nest.row + PH)[:1]
            ends.append(
                tuple(
                    take(jnp.broadcast_to(edge, (PH, COLS)), nest.spread)
                    for edge in (north, south)
                )
            )
        return ends

    def above(x, edge):
        x = pltpu.roll(x, 1, 0)
        return jnp.concatenate([jnp.where(small_row == 0, edge, x[:PH]), x[PH:]], axis=0)

    def below(x, edge):
        x = pltpu.roll(x, FR - 1, 0)
        end = jnp.where(small_row == PH - 1, edge, x[FR - PH :])
        return jnp.concatenate([x[: FR - PH], end], axis=0)

    old_ends = ghosts(0)
    for step in range(STEPS):
        old, new = step % 2, (step + 1) % 2
        surface, eastward, southward = outer_ref[0], outer_ref[1], outer_ref[2]
        flow = (eastward - pltpu.roll(eastward, 1, 1)) + (southward - pltpu.roll(southward, 1, 0))
        surface = surface - flow
        if inside is not None:
            surface = jnp.where(inside, surface, 0.0)
        to_east = pltpu.roll(surface, 2 * COLS - 1, 1)
        to_south = pltpu.roll(surface, EXT - 1, 0)
        eastward = outer_ref[5] * (
            eastward - HALF_SQUARE * (surface + to_east) * (to_east - surface)
        ) - outer_ref[3] * (to_east - surface)
        southward = outer_ref[6] * (
            southward - HALF_SQUARE * (surface + to_south) * (to_south - surface)
        ) - outer_ref[4] * (to_south - surface)
        outer_ref[0] = surface
        outer_ref[1] = eastward
        outer_ref[2] = southward
        new_ends = ghosts(new)
        for i, spot in enumerate(nests):
            level, east_flux, south_flux = (fine_ref[i, k] for k in range(3))
            old_side, new_side = rep_ref[old, i], rep_ref[new, i]
            (old_north, old_south), (new_north, new_south) = old_ends[i], new_ends[i]
            for m in range(1, RR + 1):
                part = m / RR
                side = old_side + part * (new_side - old_side)
                north = old_north + part * (new_north - old_north)
                south = old_south + part * (new_south - old_south)
                west_of = jnp.where(lane == 0, side, pltpu.roll(east_flux, 1, 1))
                north_of = above(south_flux, north)
                level = level - ((east_flux - west_of) + (south_flux - north_of))
                east_of = jnp.where(lane == COLS - 1, side, pltpu.roll(level, COLS - 1, 1))
                south_of = below(level, south)
                half_east, half_south = fine_ref[i, 5], fine_ref[i, 6]
                if step == 0 and m == 1:
                    east_flux = jnp.where(half_east == 0.0, 0.0, east_flux)
                    south_flux = jnp.where(half_south == 0.0, 0.0, south_flux)
                east_flux = east_flux - (fine_ref[i, 3] + half_east * (level + east_of)) * (
                    east_of - level
                )
                south_flux = south_flux - (fine_ref[i, 4] + half_south * (level + south_of)) * (
                    south_of - level
                )
            for k, value in enumerate((level, east_flux, south_flux)):
                fine_ref[i, k] = value

            def every(k, m):
                return fine_ref[i, k, pl.ds(m, PH, stride=RR), :]

            def quads(x):
                parts = [take(x, spot.gather + m) for m in range(RR)]
                return (parts[0] + parts[1]) + (parts[2] + parts[3])

            sum_level = (every(0, 0) + every(0, 1)) + (every(0, 2) + every(0, 3))
            sum_east = (every(1, 0) + every(1, 1)) + (every(1, 2) + every(1, 3))
            back = (
                quads(sum_level) * (1.0 / (RR * RR)),
                take(sum_east, spot.gather + (RR - 1)) * (1.0 / RR),
                quads(every(2, RR - 1)) * (1.0 / RR),
            )
            rows = pl.ds(pl.multiple_of(spot.row, 8), PH)
            for k in range(3):
                pltpu.store(outer_ref.at[k, rows, 0:COLS], back[k], mask=spot.covers)
        old_ends = new_ends

    for k in range(3):
        scale = 1.0 if k == 0 else 1.0 / COURANT
        if tile_side:
            out_ref[0, k] = outer_ref[k, HALO : HALO + ROWS, 0:COLS] * scale
        else:
            for s in range(K):
                rows = pl.ds(s * FR, FR)
                out_ref[0, k, rows, :] = jnp.where(
                    live[s], fine_ref[2 * s, k] * scale, state_ref[0, k, rows, :]
                )


def window(tile_side, units, place, host, pieces, others, state, depth, opening):
    block = UNIT * units
    nests = units if tile_side else K * 2
    table = pltpu.SMEM((PEERS * K * SPOTS,), jnp.int32)
    blocks = pl.pallas_call(
        functools.partial(compact_tiles_kernel, units) if tile_side else compact_slots_kernel,
        out_shape=jax.ShapeDtypeStruct((PEERS * block, COLS), jnp.float32),
        in_specs=[SMEM, SMEM, VMEM, VMEM],
        out_specs=VMEM,
        scratch_shapes=[table],
        compiler_params=pltpu.CompilerParams(vmem_limit_bytes=8 * 1024 * 1024),
        name="compact_tiles" if tile_side else "compact_slots",
    )(place, host, pieces.reshape(-1, COLS), others.reshape(-1, COLS))
    got = lax.all_to_all(
        blocks.reshape(PEERS, block, COLS),
        ("row", "nest"),
        split_axis=0,
        concat_axis=0,
        tiled=True,
    )
    return pl.pallas_call(
        functools.partial(window_kernel, tile_side, units),
        out_shape=jax.ShapeDtypeStruct(state.shape, jnp.float32),
        in_specs=[SMEM, SMEM, VMEM, VMEM, VMEM, VMEM],
        out_specs=VMEM,
        scratch_shapes=[
            pltpu.VMEM((CHAN, EXT, 2 * COLS), jnp.float32),
            pltpu.VMEM((nests, CHAN, FR, COLS), jnp.float32),
            pltpu.VMEM((2, nests, FR, COLS), jnp.float32),
            table,
        ],
        compiler_params=pltpu.CompilerParams(vmem_limit_bytes=32 * 1024 * 1024),
        name="window_tiles" if tile_side else "window_slots",
    )(place, host, state, depth, opening, got.reshape(-1, COLS))


def on_device(ocean_state, face_depth, face_open, nest_place, nest_host):
    tiles = ("row", "nest")
    packed, place, host, crowded = pl.pallas_call(
        pack_kernel,
        out_shape=(
            jax.ShapeDtypeStruct((PEERS * 8, COLS), jnp.float32),
            jax.ShapeDtypeStruct((1, NESTS), jnp.int32),
            jax.ShapeDtypeStruct((1, NESTS), jnp.int32),
            jax.ShapeDtypeStruct((1, 1), jnp.int32),
        ),
        in_specs=[pl.BlockSpec(memory_space=pltpu.HBM)] * 5,
        out_specs=(VMEM, VMEM, VMEM, pl.BlockSpec(memory_space=pltpu.HBM)),
        scratch_shapes=[
            pltpu.VMEM(ocean_state.shape, jnp.float32),
            pltpu.VMEM(face_depth.shape, jnp.float32),
            pltpu.VMEM(face_open.shape, jnp.int32),
            pltpu.VMEM((1, 1), jnp.int32),
            pltpu.SemaphoreType.DMA((6,)),
        ],
        compiler_params=pltpu.CompilerParams(vmem_limit_bytes=4 * 1024 * 1024),
        name="pack",
    )(*(
        pltpu.with_memory_space_constraint(x, pltpu.HBM)
        for x in (nest_place.reshape(1, NESTS), nest_host.reshape(1, NESTS), ocean_state, face_depth, face_open)
    ))
    pieces = lax.all_to_all(
        packed.reshape(PEERS, 8, COLS), tiles, split_axis=0, concat_axis=0, tiled=True
    )
    others = lax.ppermute(pieces, "sec", [(0, 1), (1, 0)])
    which = jnp.where(lax.axis_index("sec") == 0, crowded[0, 0], 2)
    return lax.switch(
        which,
        [
            functools.partial(window, True, FEW),
            functools.partial(window, True, MANY),
            functools.partial(window, False, SLOT_UNITS),
        ],
        place, host, pieces, others, ocean_state, face_depth, face_open,
    )


def solution(mesh):
    placed = (
        P("sec", None, "row", "nest"),
        P("sec", None, "row", "nest"),
        P("sec", None, "row", "nest"),
        P(),
        P(),
    )
    return jax.shard_map(
        on_device,
        mesh=mesh,
        in_specs=placed,
        out_specs=P("sec", None, "row", "nest"),
        check_vma=False,
    )
```

time: 51.4 us -> 49.7 us (0.967)
  blocking collectives: 42.2 us -> 40 us
  between operations: 0.05 us -> 0.71 us
  waiting for transfers between devices: 1.53 us -> 0.88 us
    all_to_all x1, blocking collectives: 20.2 us -> 18 us  [window(): lax.all_to_all(blocks.reshape(PEERS, block, COLS), ('row', 'nest'), split...]
    ppermute x1, waiting for transfers between devices: 1.53 us -> 0.88 us  [on_device(): others = lax.ppermute(pieces, 'sec', [(0, 1), (1, 0)])]
where the time goes in v3:
time: 49.7 us; the launch traced here: 49.5 us
  blocking collectives  40 us (80%)
  Pallas kernels  6.99 us (14%)
  waiting for transfers between devices  0.88 us (2%)
  between operations  0.71 us (1%)
  local copies, waits for them, and re-layouts  0.65 us (1%)
    all_to_all x1, blocking collectives, on_device(): lax.all_to_all(packed.reshape(PEERS, 8, COLS), tiles, split_axis=0, conca...  21.9 us
    all_to_all x1, blocking collectives, window(): lax.all_to_all(blocks.reshape(PEERS, block, COLS), ('row', 'nest'), split...  18 us
    pallas_call x1, Pallas kernels, window(): pl.pallas_call(functools.partial(window_kernel, tile_side, units), out_sh...  4.46 us
    pallas_call x1, Pallas kernels, on_device(): pl.pallas_call(pack_kernel, out_shape=(jax.ShapeDtypeStruct((PEERS * 8, C...  1.33 us
    pallas_call x1, Pallas kernels, window(): pl.pallas_call(functools.partial(compact_tiles_kernel, units) if tile_sid...  1.2 us
  transfers between devices with their start and end apart: 1, of which 1 were waited for; matrix products, arithmetic and copies ran while one was open for 0% of the time, Pallas kernels for 0%

profile of v3, /device:TPU:0, one launch (start us, length us, event | category | flops | bytes accessed | tf_op | source)
XLA Modules:
  0.0 49.5 jit_solution(15881741385919336537)
XLA Ops:
  0.0 1.3 %pack.1 = (f32[512,128]{1,0:T(8,128)S(1)}, s32[1,64]{1,0:T(1,128)S(1)}, s32[1,64]{1,0:T(1,128)S(1)}, s32[1,1]{1,0:T(1,128)}) custom-call(s32[1,64]{1,0:T(1,128)} %bitcast.29, s32[1,64]{1,0:T(1,128)} %bitcast.30, f32[1,3,64,128]{3,2,1,0:T(8,128)} %state_in.1, f32[1,2,64,128]{3,2,1,0:T(8,128)} %depth_in.1, s32[1,2,64,128]{3,2,1,0:T(8,128)} %open_in.1), custom_call_target="tpu_custom_call" | custom-call | tf_op jit(solution)/shard_map/pack/pallas_call | solution.py:568
  1.3 0.0 copy-start
  1.3 0.0 copy-start.1
  1.4 0.0 copy-start.2
  1.4 21.9 %all_to_all.20 = f32[64,8,128]{2,1,0:T(8,128)S(1)} all-to-all(f32[64,8,128]{2,1,0:T(8,128)S(1)} %bitcast.22), channel_id=1, replica_groups=mesh['sec'=2,'row'=8,'nest'=8] {'row','nest'}, dimensions={0} | all-to-all | bytes 524288 | tf_op jit(solution)/shard_map/all_to_all | solution.py:591
  23.3 0.0 collective-permute-start
  24.0 0.9 %collective-permute-done = f32[64,8,128]{2,1,0:T(8,128)S(1)} collective-permute-done((f32[64,8,128]{2,1,0:T(8,128)S(1)}, f32[64,8,128]{2,1,0:T(8,128)S(1)}, u32[]{:S(2)}, u32[]{:S(2)}) %collective-permute-start) | collective-permute-done | bytes 262176 | tf_op jit(solution)/shard_map/ppermute | solution.py:594
  24.9 0.0 copy-done
  24.9 0.0 copy-done.1
  24.9 0.0 copy-done.2
  24.9 23.9 %conditional.1 = (f32[1,3,64,128]{3,2,1,0:T(8,128)S(1)}) conditional(s32[]{:T(128)} %clamp.3, (f32[64,8,128]{2,1,0:T(8,128)S(1)}, f32[64,8,128]{2,1,0:T(8,128)S(1)}, s32[1,64]{1,0:T(1,128)S(1)}, s32[1,64]{1,0:T(1,128)S(1)}, f32[1,3,64,128]{3,2,1,0:T(8,128)S(1)}, /*index=5*/f32[1,2,64,128]{3,2,1,0:T(8,128)S(1)}, ...), branch_computations={%region_0.1_spmd, %region_1.2_spmd, %region_2.3_spmd} | conditional | bytes 1572872 | solution.py:596
  24.9 1.2 %compact_tiles.2 = f32[1024,128]{1,0:T(8,128)S(1)} custom-call(s32[1,64]{1,0:T(1,128)S(1)} %get-tuple-element.50.place_ref, s32[1,64]{1,0:T(1,128)S(1)} %get-tuple-element.52.host_ref, f32[512,128]{1,0:T(8,128)S(1)} %bitcast.23, f32[512,128]{1,0:T(8,128)S(1)} %bitcast.26), custom_call_target="tpu_custom_call" | custom-call | tf_op jit(solution)/shard_map/cond/branch_0_fun/compact_tiles/pallas_call | solution.py:534
  26.1 18.0 %all_to_all.17 = f32[64,16,128]{2,1,0:T(8,128)S(1)} all-to-all(f32[64,16,128]{2,1,0:T(8,128)S(1)} %bitcast.18), channel_id=1, replica_groups=mesh['sec'=2,'row'=8,'nest'=8] {'row','nest'}, dimensions={0} | all-to-all | bytes 1048576 | tf_op jit(solution)/shard_map/cond/branch_0_fun/all_to_all | solution.py:543
  44.1 4.5 %window_tiles.2 = f32[1,3,64,128]{3,2,1,0:T(8,128)S(1)} custom-call(s32[1,64]{1,0:T(1,128)S(1)} %get-tuple-element.50.place_ref, s32[1,64]{1,0:T(1,128)S(1)} %get-tuple-element.52.host_ref, f32[1,3,64,128]{3,2,1,0:T(8,128)S(1)} %get-tuple-element.53.state_ref, f32[1,2,64,128]{3,2,1,0:T(8,128)S(1)} %get-tuple-element.54.depth_ref, ...), custom_call_target="tpu_custom_call" | custom-call | tf_op jit(solution)/shard_map/cond/branch_0_fun/window_tiles/pallas_call | solution.py:550
  48.8 0.0 copy-start.3
  48.8 0.6 %copy-done.3 = f32[1,3,64,128]{3,2,1,0:T(8,128)} copy-done((f32[1,3,64,128]{3,2,1,0:T(8,128)}, f32[1,3,64,128]{3,2,1,0:T(8,128)S(1)}, u32[]{:S(2)}) %copy-start.3) | copy-done | bytes 98328
Async XLA Ops:
  1.3 23.5 %copy-start = (f32[1,3,64,128]{3,2,1,0:T(8,128)S(1)}, f32[1,3,64,128]{3,2,1,0:T(8,128)}, u32[]{:S(2)}) copy-start(f32[1,3,64,128]{3,2,1,0:T(8,128)} %state_in.1) | copy-start | bytes 294916
  1.3 23.5 %copy-start.1 = (f32[1,2,64,128]{3,2,1,0:T(8,128)S(1)}, f32[1,2,64,128]{3,2,1,0:T(8,128)}, u32[]{:S(2)}) copy-start(f32[1,2,64,128]{3,2,1,0:T(8,128)} %depth_in.1) | copy-start | bytes 196612
  1.4 23.5 %copy-start.2 = (s32[1,2,64,128]{3,2,1,0:T(8,128)S(1)}, s32[1,2,64,128]{3,2,1,0:T(8,128)}, u32[]{:S(2)}) copy-start(s32[1,2,64,128]{3,2,1,0:T(8,128)} %open_in.1) | copy-start | bytes 196612
  23.3 1.5 %collective-permute-start = (f32[64,8,128]{2,1,0:T(8,128)S(1)}, f32[64,8,128]{2,1,0:T(8,128)S(1)}, u32[]{:S(2)}, u32[]{:S(2)}) collective-permute-start(f32[64,8,128]{2,1,0:T(8,128)S(1)} %all_to_all.20), channel_id=1, source_target_pairs={{0,64},{64,0},{1,65},{65,1},{2,66},{66,2},{3,67},{67,3},{4,68},{68... | collective-permute-start | bytes 786440 | tf_op jit(solution)/shard_map/ppermute | solution.py:594
  48.8 0.6 %copy-start.3 = (f32[1,3,64,128]{3,2,1,0:T(8,128)}, f32[1,3,64,128]{3,2,1,0:T(8,128)S(1)}, u32[]{:S(2)}) copy-start(f32[1,3,64,128]{3,2,1,0:T(8,128)S(1)} %get-tuple-element.86) | copy-start | bytes 294916

commit v4 on v3

--- a/solution.py
+++ b/solution.py
@@ -49,8 +49,7 @@
 
 def pack_kernel(
     place_in, host_in, state_in, depth_in, open_in,
-    out_ref, place_ref, host_ref, crowded_out,
-    state_ref, depth_ref, open_ref, crowded_ref, sems,
+    out_ref, place_ref, host_ref, state_ref, depth_ref, open_ref, sems,
 ):
     moves = [
         pltpu.make_async_copy(source, target, sems.at[i])
@@ -63,15 +62,7 @@
     ]
     for move in moves:
         move.start()
-    for move in moves[:2]:
-        move.wait()
-    tile = lax.broadcasted_iota(jnp.int32, (PEERS, NESTS), 0)
-    hits = jnp.where(div6(place_ref[...]) == tile, 1.0, 0.0)
-    most = jnp.max(jnp.sum(hits, axis=1, keepdims=True), axis=0, keepdims=True)
-    crowded_ref[...] = jnp.where(most > FEW, 1, 0)
-    report = pltpu.make_async_copy(crowded_ref, crowded_out, sems.at[len(moves)])
-    report.start()
-    for move in moves[2:]:
+    for move in moves:
         move.wait()
 
     def channel(k, rows):
@@ -101,7 +92,13 @@
             if b == 0:
                 rim = pltpu.roll(rim, HALF, 1)
             out_ref[pl.ds(base + PART, FR, stride=8), :] = jnp.where(left, half, rim)
-    report.wait()
+
+
+def count_kernel(place_ref, pieces_ref, crowded_ref):
+    tile = lax.broadcasted_iota(jnp.int32, (PEERS, NESTS), 0)
+    hits = jnp.where(div6(place_ref[...]) == tile, 1.0, 0.0)
+    most = jnp.max(jnp.sum(hits, axis=1, keepdims=True), axis=0, keepdims=True)
+    crowded_ref[...] = jnp.where(most > FEW, 1, 0)
 
 
 def clear_table(table_ref, first, count, value=-1):
@@ -112,10 +109,9 @@
 def compact_tiles_kernel(units, place_ref, host_ref, own_ref, other_ref, out_ref, table_ref):
     block = UNIT * units
     me = lax.axis_index("row") * lax.axis_size("nest") + lax.axis_index("nest")
-    sub = lax.broadcasted_iota(jnp.int32, (8, COLS), 0)
-    sub_lane = lax.broadcasted_iota(jnp.int32, (8, COLS), 1)
-    used = (sub_lane < HALF) | ((sub & (UNIT - 1)) < PART)
-    half_of = jnp.where(used, jnp.where(sub < UNIT, 0, 1), 2)
+    used = (lax.broadcasted_iota(jnp.int32, (UNIT, COLS), 1) < HALF) | (
+        lax.broadcasted_iota(jnp.int32, (UNIT, COLS), 0) < PART
+    )
 
     out_ref[...] = jnp.zeros_like(out_ref)
     clear_table(table_ref, 0, PEERS, 0)
@@ -125,13 +121,12 @@
         t = div6(place_ref[0, n])
         u = table_ref[t]
         table_ref[t] = u + 1
-        piece = other_ref[pl.ds(pl.multiple_of((h >> 1) * 8, 8), 8), :]
-        piece = jnp.where((h & 1) != (u & 1), pltpu.roll(piece, UNIT, 0), piece)
-        spot = pl.ds(pl.multiple_of(t * block + (u >> 1) * 8, 8), 8)
-        pltpu.store(out_ref.at[spot, :], piece, mask=half_of == (u & 1))
+        piece = other_ref[pl.ds(pl.multiple_of(h * UNIT, UNIT), UNIT), :]
+        spot = pl.ds(pl.multiple_of(t * block + u * UNIT, UNIT), UNIT)
+        pltpu.store(out_ref.at[spot, :], piece, mask=used)
         return carry
 
-    lax.fori_loop(0, NESTS, place_one, 0, unroll=8)
+    lax.fori_loop(0, NESTS, place_one, 0, unroll=16)
 
     tile = lax.broadcasted_iota(jnp.int32, (PEERS, COLS), 0)
     lane = lax.broadcasted_iota(jnp.int32, (PEERS, COLS), 1)
@@ -184,17 +179,14 @@
 
 def compact_slots_kernel(place_ref, host_ref, own_ref, other_ref, out_ref, table_ref):
     me = lax.axis_index("row") * lax.axis_size("nest") + lax.axis_index("nest")
-    sub = lax.broadcasted_iota(jnp.int32, (8, COLS), 0)
-    lane = lax.broadcasted_iota(jnp.int32, (8, COLS), 1)
-    whole = (sub & (UNIT - 1)) < PART
-    half_of = jnp.where(sub < UNIT, 0, 1)
+    lane = lax.broadcasted_iota(jnp.int32, (UNIT, COLS), 1)
+    whole = lax.broadcasted_iota(jnp.int32, (UNIT, COLS), 0) < PART
     is_outer = jnp.where(whole, jnp.where((lane >= PW) & (lane < COLS - PW), 1, 0), 0)
     is_outer = jnp.where(whole | (lane < HALF), is_outer, 1)
     is_east = jnp.where(whole, jnp.where(lane < HALF, 1, 0), jnp.where(me < FR, 1, 0))
 
     def unit(source_ref, i):
-        piece = source_ref[pl.ds(pl.multiple_of((i >> 1) * 8, 8), 8), :]
-        return jnp.where(half_of == (i & 1), piece, pltpu.roll(piece, UNIT, 0))
+        return source_ref[pl.ds(pl.multiple_of(i * UNIT, UNIT), UNIT), :]
 
     def clear(n, carry):
         clear_table(table_ref, 3 * div3(place_ref[0, n]), SPOTS, 0)
@@ -217,14 +209,13 @@
         )
         outer = jnp.where(whole, moved, pltpu.roll(outer, HALF, 1))
         value = jnp.where(is_outer == 1, outer, jnp.where(is_east == 1, east, west))
-        spot = pl.ds(pl.multiple_of((h >> 1) * 8, 8), 8)
-        pltpu.store(out_ref.at[spot, :], value, mask=half_of == (h & 1))
+        out_ref[pl.ds(pl.multiple_of(h * UNIT, UNIT), UNIT), :] = value
         return carry
 
     out_ref[...] = jnp.zeros_like(out_ref)
     lax.fori_loop(0, NESTS, clear, 0, unroll=8)
     lax.fori_loop(0, NESTS, note, 0, unroll=8)
-    lax.fori_loop(0, NESTS, gather_band, 0, unroll=4)
+    lax.fori_loop(0, NESTS, gather_band, 0, unroll=8)
 
 
 class Nest(NamedTuple):
@@ -565,22 +556,20 @@
 
 def on_device(ocean_state, face_depth, face_open, nest_place, nest_host):
     tiles = ("row", "nest")
-    packed, place, host, crowded = pl.pallas_call(
+    packed, place, host = pl.pallas_call(
         pack_kernel,
         out_shape=(
             jax.ShapeDtypeStruct((PEERS * 8, COLS), jnp.float32),
             jax.ShapeDtypeStruct((1, NESTS), jnp.int32),
             jax.ShapeDtypeStruct((1, NESTS), jnp.int32),
-            jax.ShapeDtypeStruct((1, 1), jnp.int32),
         ),
         in_specs=[pl.BlockSpec(memory_space=pltpu.HBM)] * 5,
-        out_specs=(VMEM, VMEM, VMEM, pl.BlockSpec(memory_space=pltpu.HBM)),
+        out_specs=(VMEM, VMEM, VMEM),
         scratch_shapes=[
             pltpu.VMEM(ocean_state.shape, jnp.float32),
             pltpu.VMEM(face_depth.shape, jnp.float32),
             pltpu.VMEM(face_open.shape, jnp.int32),
-            pltpu.VMEM((1, 1), jnp.int32),
-            pltpu.SemaphoreType.DMA((6,)),
+            pltpu.SemaphoreType.DMA((5,)),
         ],
         compiler_params=pltpu.CompilerParams(vmem_limit_bytes=4 * 1024 * 1024),
         name="pack",
@@ -592,6 +581,14 @@
         packed.reshape(PEERS, 8, COLS), tiles, split_axis=0, concat_axis=0, tiled=True
     )
     others = lax.ppermute(pieces, "sec", [(0, 1), (1, 0)])
+    crowded = pl.pallas_call(
+        count_kernel,
+        out_shape=jax.ShapeDtypeStruct((1, 1), jnp.int32),
+        in_specs=[VMEM, pl.BlockSpec(memory_space=pl.ANY)],
+        out_specs=VMEM,
+        compiler_params=pltpu.CompilerParams(vmem_limit_bytes=4 * 1024 * 1024),
+        name="count",
+    )(place, pieces)
     which = jnp.where(lax.axis_index("sec") == 0, crowded[0, 0], 2)
     return lax.switch(
         which,

time: 49.7 us -> 48.9 us (0.984)
  waiting for transfers between devices: 0.88 us -> 0.26 us
    ppermute x1, waiting for transfers between devices: 0.88 us -> 0.26 us  [on_device(): others = lax.ppermute(pieces, 'sec', [(0, 1), (1, 0)])]
    pallas_call x0 -> x1, Pallas kernels: none -> 0.61 us  [on_device(): pl.pallas_call(count_kernel, out_shape=jax.ShapeDtypeStruct((1, 1), jnp.i...]
  transfers between devices with their start and end apart: 1 -> 1, of which waited for: 1 -> 1; matrix products, arithmetic and copies ran while one was open for 0% -> 0% of each run, Pallas kernels for 0% -> 1%
where the time goes in v4:
time: 48.9 us; the launch traced here: 48.7 us
  blocking collectives  39.6 us (81%)
  Pallas kernels  7.25 us (15%)
  between operations  0.69 us (1%)
  local copies, waits for them, and re-layouts  0.65 us (1%)
    all_to_all x1, blocking collectives, on_device(): lax.all_to_all(packed.reshape(PEERS, 8, COLS), tiles, split_axis=0, conca...  21.8 us
    all_to_all x1, blocking collectives, window(): lax.all_to_all(blocks.reshape(PEERS, block, COLS), ('row', 'nest'), split...  17.8 us
    pallas_call x1, Pallas kernels, window(): pl.pallas_call(functools.partial(window_kernel, tile_side, units), out_sh...  4.46 us
    pallas_call x1, Pallas kernels, on_device(): pl.pallas_call(pack_kernel, out_shape=(jax.ShapeDtypeStruct((PEERS * 8, C...  1.11 us
    pallas_call x1, Pallas kernels, window(): pl.pallas_call(functools.partial(compact_tiles_kernel, units) if tile_sid...  1.07 us
  transfers between devices with their start and end apart: 1, of which 1 were waited for; matrix products, arithmetic and copies ran while one was open for 0% of the time, Pallas kernels for 1%

profile of v4, /device:TPU:0, one launch (start us, length us, event | category | flops | bytes accessed | tf_op | source)
XLA Modules:
  0.0 48.7 jit_solution(14949905023416809866)
XLA Ops:
  0.0 1.1 %pack.1 = (f32[512,128]{1,0:T(8,128)S(1)}, s32[1,64]{1,0:T(1,128)S(1)}, s32[1,64]{1,0:T(1,128)S(1)}) custom-call(s32[1,64]{1,0:T(1,128)} %bitcast.29, s32[1,64]{1,0:T(1,128)} %bitcast.30, f32[1,3,64,128]{3,2,1,0:T(8,128)} %state_in.1, f32[1,2,64,128]{3,2,1,0:T(8,128)} %depth_in.1, s32[1,2,64,128]{3,2,1,0:T(8,128)} %open_in.1), custom_call_target="tpu_custom_call" | custom-call | tf_op jit(solution)/shard_map/pack/pallas_call | solution.py:559
  1.1 21.8 %all_to_all.20.pieces_ref = f32[64,8,128]{2,1,0:T(8,128)S(1)} all-to-all(f32[64,8,128]{2,1,0:T(8,128)S(1)} %bitcast.22), channel_id=1, replica_groups=mesh['sec'=2,'row'=8,'nest'=8] {'row','nest'}, dimensions={0} | all-to-all | bytes 524288 | tf_op jit(solution)/shard_map/all_to_all | solution.py:580
  22.9 0.0 collective-permute-start
  22.9 0.0 copy-start
  22.9 0.0 copy-start.1
  22.9 0.0 copy-start.2
  22.9 0.6 %count.1 = s32[1,1]{1,0:T(1,128)} custom-call(s32[1,64]{1,0:T(1,128)S(1)} %get-tuple-element.75.place_ref, f32[64,8,128]{2,1,0:T(8,128)S(1)} %all_to_all.20.pieces_ref), custom_call_target="tpu_custom_call" | custom-call | tf_op jit(solution)/shard_map/count/pallas_call | solution.py:584
  24.2 0.3 collective-permute-done
  24.5 0.0 copy-done
  24.5 0.0 copy-done.1
  24.5 0.0 copy-done.2
  24.5 23.5 %conditional.1 = (f32[1,3,64,128]{3,2,1,0:T(8,128)S(1)}) conditional(s32[]{:T(128)} %clamp.3, (f32[64,8,128]{2,1,0:T(8,128)S(1)}, f32[64,8,128]{2,1,0:T(8,128)S(1)}, s32[1,64]{1,0:T(1,128)S(1)}, s32[1,64]{1,0:T(1,128)S(1)}, f32[1,3,64,128]{3,2,1,0:T(8,128)S(1)}, /*index=5*/f32[1,2,64,128]{3,2,1,0:T(8,128)S(1)}, ...), branch_computations={%region_0.1_spmd, %region_1.2_spmd, %region_2.3_spmd} | conditional | bytes 1572872 | solution.py:593
  24.5 1.1 %compact_tiles.2 = f32[1024,128]{1,0:T(8,128)S(1)} custom-call(s32[1,64]{1,0:T(1,128)S(1)} %get-tuple-element.50.place_ref, s32[1,64]{1,0:T(1,128)S(1)} %get-tuple-element.52.host_ref, f32[512,128]{1,0:T(8,128)S(1)} %bitcast.23, f32[512,128]{1,0:T(8,128)S(1)} %bitcast.26), custom_call_target="tpu_custom_call" | custom-call | tf_op jit(solution)/shard_map/cond/branch_0_fun/compact_tiles/pallas_call | solution.py:525
  25.6 17.8 %all_to_all.17 = f32[64,16,128]{2,1,0:T(8,128)S(1)} all-to-all(f32[64,16,128]{2,1,0:T(8,128)S(1)} %bitcast.18), channel_id=1, replica_groups=mesh['sec'=2,'row'=8,'nest'=8] {'row','nest'}, dimensions={0} | all-to-all | bytes 1048576 | tf_op jit(solution)/shard_map/cond/branch_0_fun/all_to_all | solution.py:534
  43.3 4.5 %window_tiles.2 = f32[1,3,64,128]{3,2,1,0:T(8,128)S(1)} custom-call(s32[1,64]{1,0:T(1,128)S(1)} %get-tuple-element.50.place_ref, s32[1,64]{1,0:T(1,128)S(1)} %get-tuple-element.52.host_ref, f32[1,3,64,128]{3,2,1,0:T(8,128)S(1)} %get-tuple-element.53.state_ref, f32[1,2,64,128]{3,2,1,0:T(8,128)S(1)} %get-tuple-element.54.depth_ref, ...), custom_call_target="tpu_custom_call" | custom-call | tf_op jit(solution)/shard_map/cond/branch_0_fun/window_tiles/pallas_call | solution.py:541
  48.0 0.0 copy-start.3
  48.0 0.6 %copy-done.3 = f32[1,3,64,128]{3,2,1,0:T(8,128)} copy-done((f32[1,3,64,128]{3,2,1,0:T(8,128)}, f32[1,3,64,128]{3,2,1,0:T(8,128)S(1)}, u32[]{:S(2)}) %copy-start.3) | copy-done | bytes 98328
Async XLA Ops:
  22.9 1.5 %collective-permute-start = (f32[64,8,128]{2,1,0:T(8,128)S(1)}, f32[64,8,128]{2,1,0:T(8,128)S(1)}, u32[]{:S(2)}, u32[]{:S(2)}) collective-permute-start(f32[64,8,128]{2,1,0:T(8,128)S(1)} %all_to_all.20.pieces_ref), channel_id=1, source_target_pairs={{0,64},{64,0},{1,65},{65,1},{2,66},{66,2},{3,67},{67,3},{4,68},{68... | collective-permute-start | bytes 786440 | tf_op jit(solution)/shard_map/ppermute | solution.py:583
  22.9 1.5 %copy-start = (f32[1,3,64,128]{3,2,1,0:T(8,128)S(1)}, f32[1,3,64,128]{3,2,1,0:T(8,128)}, u32[]{:S(2)}) copy-start(f32[1,3,64,128]{3,2,1,0:T(8,128)} %state_in.1) | copy-start | bytes 294916
  22.9 1.5 %copy-start.1 = (f32[1,2,64,128]{3,2,1,0:T(8,128)S(1)}, f32[1,2,64,128]{3,2,1,0:T(8,128)}, u32[]{:S(2)}) copy-start(f32[1,2,64,128]{3,2,1,0:T(8,128)} %depth_in.1) | copy-start | bytes 196612
  22.9 1.5 %copy-start.2 = (s32[1,2,64,128]{3,2,1,0:T(8,128)S(1)}, s32[1,2,64,128]{3,2,1,0:T(8,128)}, u32[]{:S(2)}) copy-start(s32[1,2,64,128]{3,2,1,0:T(8,128)} %open_in.1) | copy-start | bytes 196612
  48.0 0.6 %copy-start.3 = (f32[1,3,64,128]{3,2,1,0:T(8,128)}, f32[1,3,64,128]{3,2,1,0:T(8,128)S(1)}, u32[]{:S(2)}) copy-start(f32[1,3,64,128]{3,2,1,0:T(8,128)S(1)} %get-tuple-element.84) | copy-start | bytes 294916

commit v5 on v4

--- a/solution.py
+++ b/solution.py
@@ -94,39 +94,12 @@
             out_ref[pl.ds(base + PART, FR, stride=8), :] = jnp.where(left, half, rim)
 
 
-def count_kernel(place_ref, pieces_ref, crowded_ref):
-    tile = lax.broadcasted_iota(jnp.int32, (PEERS, NESTS), 0)
-    hits = jnp.where(div6(place_ref[...]) == tile, 1.0, 0.0)
+def prepare_kernel(place_ref, own_ref, crowded_ref, halo_ref):
+    me = lax.axis_index("row") * lax.axis_size("nest") + lax.axis_index("nest")
+    hit_tile = lax.broadcasted_iota(jnp.int32, (PEERS, NESTS), 0)
+    hits = jnp.where(div6(place_ref[...]) == hit_tile, 1.0, 0.0)
     most = jnp.max(jnp.sum(hits, axis=1, keepdims=True), axis=0, keepdims=True)
     crowded_ref[...] = jnp.where(most > FEW, 1, 0)
-
-
-def clear_table(table_ref, first, count, value=-1):
-    for i in range(count):
-        table_ref[first + i] = value
-
-
-def compact_tiles_kernel(units, place_ref, host_ref, own_ref, other_ref, out_ref, table_ref):
-    block = UNIT * units
-    me = lax.axis_index("row") * lax.axis_size("nest") + lax.axis_index("nest")
-    used = (lax.broadcasted_iota(jnp.int32, (UNIT, COLS), 1) < HALF) | (
-        lax.broadcasted_iota(jnp.int32, (UNIT, COLS), 0) < PART
-    )
-
-    out_ref[...] = jnp.zeros_like(out_ref)
-    clear_table(table_ref, 0, PEERS, 0)
-
-    def place_one(n, carry):
-        h = host_ref[0, n]
-        t = div6(place_ref[0, n])
-        u = table_ref[t]
-        table_ref[t] = u + 1
-        piece = other_ref[pl.ds(pl.multiple_of(h * UNIT, UNIT), UNIT), :]
-        spot = pl.ds(pl.multiple_of(t * block + u * UNIT, UNIT), UNIT)
-        pltpu.store(out_ref.at[spot, :], piece, mask=used)
-        return carry
-
-    lax.fori_loop(0, NESTS, place_one, 0, unroll=16)
 
     tile = lax.broadcasted_iota(jnp.int32, (PEERS, COLS), 0)
     lane = lax.broadcasted_iota(jnp.int32, (PEERS, COLS), 1)
@@ -173,8 +146,39 @@
     left = jnp.where(has_left & (lane >= COLS - HALO), left_of(rims[1]), 0.0)
     packed += pltpu.roll(right, HALF - HALO, 1) + pltpu.roll(left, COLS - HALO, 1)
     for u, value in enumerate([packed] + rims):
+        halo_ref[u] = value
+
+
+def clear_table(table_ref, first, count, value=-1):
+    for i in range(count):
+        table_ref[first + i] = value
+
+
+def compact_tiles_kernel(units, place_ref, host_ref, halo_ref, other_ref, out_ref, table_ref):
+    block = UNIT * units
+    used = (lax.broadcasted_iota(jnp.int32, (UNIT, COLS), 1) < HALF) | (
+        lax.broadcasted_iota(jnp.int32, (UNIT, COLS), 0) < PART
+    )
+
+    out_ref[...] = jnp.zeros_like(out_ref)
+    clear_table(table_ref, 0, PEERS, 0)
+
+    def place_one(n, carry):
+        h = host_ref[0, n]
+        t = div6(place_ref[0, n])
+        u = table_ref[t]
+        table_ref[t] = u + 1
+        piece = other_ref[pl.ds(pl.multiple_of(h * UNIT, UNIT), UNIT), :]
+        spot = pl.ds(pl.multiple_of(t * block + u * UNIT, UNIT), UNIT)
+        pltpu.store(out_ref.at[spot, :], piece, mask=used)
+        return carry
+
+    lax.fori_loop(0, NESTS, place_one, 0, unroll=True)
+
+    lane = lax.broadcasted_iota(jnp.int32, (PEERS, COLS), 1)
+    for u in range(SPOTS):
         spot = pl.ds(UNIT * u + PART, PEERS, stride=block)
-        out_ref[spot, :] = jnp.where(lane >= HALF, value, out_ref[spot, :])
+        out_ref[spot, :] = jnp.where(lane >= HALF, halo_ref[u], out_ref[spot, :])
 
 
 def compact_slots_kernel(place_ref, host_ref, own_ref, other_ref, out_ref, table_ref):
@@ -274,7 +278,7 @@
             table_ref[count] = p - 6 * me
             return count + jnp.where(div6(p) == me, 1, 0)
 
-        count = lax.fori_loop(0, NESTS, find, 0, unroll=16)
+        count = lax.fori_loop(0, NESTS, find, 0, unroll=True)
         nests = []
         for u in range(units):
             p = jnp.where(u < count, table_ref[u], 0)
@@ -518,7 +522,7 @@
                 )
 
 
-def window(tile_side, units, place, host, pieces, others, state, depth, opening):
+def window(tile_side, units, place, host, pieces, halos, others, state, depth, opening):
     block = UNIT * units
     nests = units if tile_side else K * 2
     table = pltpu.SMEM((PEERS * K * SPOTS,), jnp.int32)
@@ -530,7 +534,7 @@
         scratch_shapes=[table],
         compiler_params=pltpu.CompilerParams(vmem_limit_bytes=8 * 1024 * 1024),
         name="compact_tiles" if tile_side else "compact_slots",
-    )(place, host, pieces.reshape(-1, COLS), others.reshape(-1, COLS))
+    )(place, host, halos if tile_side else pieces.reshape(-1, COLS), others.reshape(-1, COLS))
     got = lax.all_to_all(
         blocks.reshape(PEERS, block, COLS),
         ("row", "nest"),
@@ -581,14 +585,17 @@
         packed.reshape(PEERS, 8, COLS), tiles, split_axis=0, concat_axis=0, tiled=True
     )
     others = lax.ppermute(pieces, "sec", [(0, 1), (1, 0)])
-    crowded = pl.pallas_call(
-        count_kernel,
-        out_shape=jax.ShapeDtypeStruct((1, 1), jnp.int32),
-        in_specs=[VMEM, pl.BlockSpec(memory_space=pl.ANY)],
-        out_specs=VMEM,
+    crowded, halos = pl.pallas_call(
+        prepare_kernel,
+        out_shape=(
+            jax.ShapeDtypeStruct((1, 1), jnp.int32),
+            jax.ShapeDtypeStruct((SPOTS, PEERS, COLS), jnp.float32),
+        ),
+        in_specs=[VMEM, VMEM],
+        out_specs=(VMEM, VMEM),
         compiler_params=pltpu.CompilerParams(vmem_limit_bytes=4 * 1024 * 1024),
-        name="count",
-    )(place, pieces)
+        name="prepare",
+    )(place, pieces.reshape(-1, COLS))
     which = jnp.where(lax.axis_index("sec") == 0, crowded[0, 0], 2)
     return lax.switch(
         which,
@@ -597,7 +604,7 @@
             functools.partial(window, True, MANY),
             functools.partial(window, False, SLOT_UNITS),
         ],
-        place, host, pieces, others, ocean_state, face_depth, face_open,
+        place, host, pieces, halos, others, ocean_state, face_depth, face_open,
     )
 
 

time: 48.9 us -> 48.7 us (level)
  no operation moved by 1% of the time
where the time goes in v5:
time: 48.7 us; the launch traced here: 48.5 us
  blocking collectives  39.8 us (82%)
  Pallas kernels  6.94 us (14%)
  between operations  0.69 us (1%)
  local copies, waits for them, and re-layouts  0.65 us (1%)
    all_to_all x1, blocking collectives, on_device(): lax.all_to_all(packed.reshape(PEERS, 8, COLS), tiles, split_axis=0, conca...  21.8 us
    all_to_all x1, blocking collectives, window(): lax.all_to_all(blocks.reshape(PEERS, block, COLS), ('row', 'nest'), split...  17.9 us
    pallas_call x1, Pallas kernels, window(): pl.pallas_call(functools.partial(window_kernel, tile_side, units), out_sh...  4.31 us
    pallas_call x1, Pallas kernels, on_device(): pl.pallas_call(pack_kernel, out_shape=(jax.ShapeDtypeStruct((PEERS * 8, C...  1.11 us
  transfers between devices with their start and end apart: 1, of which 1 were waited for; matrix products, arithmetic and copies ran while one was open for 0% of the time, Pallas kernels for 1%

profile of v5, /device:TPU:0, one launch (start us, length us, event | category | flops | bytes accessed | tf_op | source)
XLA Modules:
  0.0 48.5 jit_solution(17029746802958389870)
XLA Ops:
  0.0 1.1 %pack.1 = (f32[512,128]{1,0:T(8,128)S(1)}, s32[1,64]{1,0:T(1,128)S(1)}, s32[1,64]{1,0:T(1,128)S(1)}) custom-call(s32[1,64]{1,0:T(1,128)} %bitcast.27, s32[1,64]{1,0:T(1,128)} %bitcast.28, f32[1,3,64,128]{3,2,1,0:T(8,128)} %state_in.1, f32[1,2,64,128]{3,2,1,0:T(8,128)} %depth_in.1, s32[1,2,64,128]{3,2,1,0:T(8,128)} %open_in.1), custom_call_target="tpu_custom_call" | custom-call | tf_op jit(solution)/shard_map/pack/pallas_call | solution.py:563
  1.1 21.8 %all_to_all.20 = f32[64,8,128]{2,1,0:T(8,128)S(1)} all-to-all(f32[64,8,128]{2,1,0:T(8,128)S(1)} %bitcast.21), channel_id=1, replica_groups=mesh['sec'=2,'row'=8,'nest'=8] {'row','nest'}, dimensions={0} | all-to-all | bytes 524288 | tf_op jit(solution)/shard_map/all_to_all | solution.py:584
  22.9 0.0 collective-permute-start
  22.9 0.0 copy-start
  22.9 0.0 copy-start.1
  22.9 0.0 copy-start.2
  22.9 0.6 %prepare.1 = (s32[1,1]{1,0:T(1,128)}, f32[3,64,128]{2,1,0:T(8,128)S(1)}) custom-call(s32[1,64]{1,0:T(1,128)S(1)} %get-tuple-element.77.place_ref, f32[512,128]{1,0:T(8,128)S(1)} %bitcast.22), custom_call_target="tpu_custom_call" | custom-call | tf_op jit(solution)/shard_map/prepare/pallas_call | solution.py:588
  24.2 0.2 collective-permute-done
  24.5 0.0 copy-done
  24.5 0.0 copy-done.1
  24.5 0.0 copy-done.2
  24.5 23.4 %conditional.1 = (f32[1,3,64,128]{3,2,1,0:T(8,128)S(1)}) conditional(s32[]{:T(128)} %clamp.3, (f32[64,8,128]{2,1,0:T(8,128)S(1)}, s32[1,64]{1,0:T(1,128)S(1)}, s32[1,64]{1,0:T(1,128)S(1)}, f32[3,64,128]{2,1,0:T(8,128)S(1)}, f32[1,3,64,128]{3,2,1,0:T(8,128)S(1)}, /*index=5*/f32[1,2,64,128]{3,2,1,0:T(8,128)S(1)}, ...), branch_computations={%region_0.1_spmd, %region_1.2_spmd, %region_2.3_spmd} | conditional | bytes 1572872 | solution.py:600
  24.5 0.9 %compact_tiles.2 = f32[1024,128]{1,0:T(8,128)S(1)} custom-call(s32[1,64]{1,0:T(1,128)S(1)} %get-tuple-element.50.place_ref, s32[1,64]{1,0:T(1,128)S(1)} %get-tuple-element.52.host_ref, f32[3,64,128]{2,1,0:T(8,128)S(1)} %get-tuple-element.56.halo_ref, f32[512,128]{1,0:T(8,128)S(1)} %bitcast.24), custom_call_target="tpu_custom_call" | custom-call | tf_op jit(solution)/shard_map/cond/branch_0_fun/compact_tiles/pallas_call | solution.py:529
  25.4 17.9 %all_to_all.17 = f32[64,16,128]{2,1,0:T(8,128)S(1)} all-to-all(f32[64,16,128]{2,1,0:T(8,128)S(1)} %bitcast.18), channel_id=1, replica_groups=mesh['sec'=2,'row'=8,'nest'=8] {'row','nest'}, dimensions={0} | all-to-all | bytes 1048576 | tf_op jit(solution)/shard_map/cond/branch_0_fun/all_to_all | solution.py:538
  43.3 4.3 %window_tiles.2 = f32[1,3,64,128]{3,2,1,0:T(8,128)S(1)} custom-call(s32[1,64]{1,0:T(1,128)S(1)} %get-tuple-element.50.place_ref, s32[1,64]{1,0:T(1,128)S(1)} %get-tuple-element.52.host_ref, f32[1,3,64,128]{3,2,1,0:T(8,128)S(1)} %get-tuple-element.53.state_ref, f32[1,2,64,128]{3,2,1,0:T(8,128)S(1)} %get-tuple-element.54.depth_ref, ...), custom_call_target="tpu_custom_call" | custom-call | tf_op jit(solution)/shard_map/cond/branch_0_fun/window_tiles/pallas_call | solution.py:545
  47.9 0.0 copy-start.3
  47.9 0.6 %copy-done.3 = f32[1,3,64,128]{3,2,1,0:T(8,128)} copy-done((f32[1,3,64,128]{3,2,1,0:T(8,128)}, f32[1,3,64,128]{3,2,1,0:T(8,128)S(1)}, u32[]{:S(2)}) %copy-start.3) | copy-done | bytes 98328
Async XLA Ops:
  22.9 1.5 %collective-permute-start = (f32[64,8,128]{2,1,0:T(8,128)S(1)}, f32[64,8,128]{2,1,0:T(8,128)S(1)}, u32[]{:S(2)}, u32[]{:S(2)}) collective-permute-start(f32[64,8,128]{2,1,0:T(8,128)S(1)} %all_to_all.20), channel_id=1, source_target_pairs={{0,64},{64,0},{1,65},{65,1},{2,66},{66,2},{3,67},{67,3},{4,68},{68... | collective-permute-start | bytes 786440 | tf_op jit(solution)/shard_map/ppermute | solution.py:587
  22.9 1.5 %copy-start = (f32[1,3,64,128]{3,2,1,0:T(8,128)S(1)}, f32[1,3,64,128]{3,2,1,0:T(8,128)}, u32[]{:S(2)}) copy-start(f32[1,3,64,128]{3,2,1,0:T(8,128)} %state_in.1) | copy-start | bytes 294916
  22.9 1.5 %copy-start.1 = (f32[1,2,64,128]{3,2,1,0:T(8,128)S(1)}, f32[1,2,64,128]{3,2,1,0:T(8,128)}, u32[]{:S(2)}) copy-start(f32[1,2,64,128]{3,2,1,0:T(8,128)} %depth_in.1) | copy-start | bytes 196612
  22.9 1.5 %copy-start.2 = (s32[1,2,64,128]{3,2,1,0:T(8,128)S(1)}, s32[1,2,64,128]{3,2,1,0:T(8,128)}, u32[]{:S(2)}) copy-start(s32[1,2,64,128]{3,2,1,0:T(8,128)} %open_in.1) | copy-start | bytes 196612
  47.9 0.6 %copy-start.3 = (f32[1,3,64,128]{3,2,1,0:T(8,128)}, f32[1,3,64,128]{3,2,1,0:T(8,128)S(1)}, u32[]{:S(2)}) copy-start(f32[1,3,64,128]{3,2,1,0:T(8,128)S(1)} %get-tuple-element.88) | copy-start | bytes 294916

commit v6 on v5

--- a/solution.py
+++ b/solution.py
@@ -161,6 +161,10 @@
     )
 
     out_ref[...] = jnp.zeros_like(out_ref)
+    lane = lax.broadcasted_iota(jnp.int32, (PEERS, COLS), 1)
+    for u in range(SPOTS):
+        spot = pl.ds(UNIT * u + PART, PEERS, stride=block)
+        out_ref[spot, :] = jnp.where(lane >= HALF, halo_ref[u], 0.0)
     clear_table(table_ref, 0, PEERS, 0)
 
     def place_one(n, carry):
@@ -174,11 +178,6 @@
         return carry
 
     lax.fori_loop(0, NESTS, place_one, 0, unroll=True)
-
-    lane = lax.broadcasted_iota(jnp.int32, (PEERS, COLS), 1)
-    for u in range(SPOTS):
-        spot = pl.ds(UNIT * u + PART, PEERS, stride=block)
-        out_ref[spot, :] = jnp.where(lane >= HALF, halo_ref[u], out_ref[spot, :])
 
 
 def compact_slots_kernel(place_ref, host_ref, own_ref, other_ref, out_ref, table_ref):
@@ -217,8 +216,8 @@
         return carry
 
     out_ref[...] = jnp.zeros_like(out_ref)
-    lax.fori_loop(0, NESTS, clear, 0, unroll=8)
-    lax.fori_loop(0, NESTS, note, 0, unroll=8)
+    lax.fori_loop(0, NESTS, clear, 0, unroll=True)
+    lax.fori_loop(0, NESTS, note, 0, unroll=True)
     lax.fori_loop(0, NESTS, gather_band, 0, unroll=8)
 
 
@@ -335,14 +334,14 @@
             return carry
 
         clear_table(table_ref, K * me, K)
-        lax.fori_loop(0, NESTS, note_host, 0, unroll=16)
+        lax.fori_loop(0, NESTS, note_host, 0, unroll=True)
         at = [table_ref[K * me + s] for s in range(K)]
         live = [p >= 0 for p in at]
         bands = [3 * div3(jnp.where(live[s], at[s], 0)) for s in range(K)]
         spots = [jnp.where(live[s], at[s] - bands[s], 0) for s in range(K)]
         for s in range(K):
             clear_table(table_ref, bands[s], SPOTS)
-        lax.fori_loop(0, NESTS, note_place, 0, unroll=16)
+        lax.fori_loop(0, NESTS, note_place, 0, unroll=True)
         nests = []
         for s in range(K):
             j = spots[s]

time: 48.7 us -> 48.7 us (level)
  no operation moved by 1% of the time
where the time goes in v6:
time: 48.7 us; the launch traced here: 48.4 us
  blocking collectives  39.7 us (82%)
  Pallas kernels  6.93 us (14%)
  between operations  0.69 us (1%)
  local copies, waits for them, and re-layouts  0.65 us (1%)
    all_to_all x1, blocking collectives, on_device(): lax.all_to_all(packed.reshape(PEERS, 8, COLS), tiles, split_axis=0, conca...  21.8 us
    all_to_all x1, blocking collectives, window(): lax.all_to_all(blocks.reshape(PEERS, block, COLS), ('row', 'nest'), split...  17.9 us
    pallas_call x1, Pallas kernels, window(): pl.pallas_call(functools.partial(window_kernel, tile_side, units), out_sh...  4.31 us
    pallas_call x1, Pallas kernels, on_device(): pl.pallas_call(pack_kernel, out_shape=(jax.ShapeDtypeStruct((PEERS * 8, C...  1.11 us
  transfers between devices with their start and end apart: 1, of which 1 were waited for; matrix products, arithmetic and copies ran while one was open for 0% of the time, Pallas kernels for 1%

profile of v6, /device:TPU:0, one launch (start us, length us, event | category | flops | bytes accessed | tf_op | source)
XLA Modules:
  0.0 48.4 jit_solution(979937446950850491)
XLA Ops:
  0.0 1.1 %pack.1 = (f32[512,128]{1,0:T(8,128)S(1)}, s32[1,64]{1,0:T(1,128)S(1)}, s32[1,64]{1,0:T(1,128)S(1)}) custom-call(s32[1,64]{1,0:T(1,128)} %bitcast.27, s32[1,64]{1,0:T(1,128)} %bitcast.28, f32[1,3,64,128]{3,2,1,0:T(8,128)} %state_in.1, f32[1,2,64,128]{3,2,1,0:T(8,128)} %depth_in.1, s32[1,2,64,128]{3,2,1,0:T(8,128)} %open_in.1), custom_call_target="tpu_custom_call" | custom-call | tf_op jit(solution)/shard_map/pack/pallas_call | solution.py:562
  1.1 21.8 %all_to_all.20 = f32[64,8,128]{2,1,0:T(8,128)S(1)} all-to-all(f32[64,8,128]{2,1,0:T(8,128)S(1)} %bitcast.21), channel_id=1, replica_groups=mesh['sec'=2,'row'=8,'nest'=8] {'row','nest'}, dimensions={0} | all-to-all | bytes 524288 | tf_op jit(solution)/shard_map/all_to_all | solution.py:583
  22.9 0.0 collective-permute-start
  22.9 0.0 copy-start
  22.9 0.0 copy-start.1
  22.9 0.0 copy-start.2
  22.9 0.6 %prepare.1 = (s32[1,1]{1,0:T(1,128)}, f32[3,64,128]{2,1,0:T(8,128)S(1)}) custom-call(s32[1,64]{1,0:T(1,128)S(1)} %get-tuple-element.77.place_ref, f32[512,128]{1,0:T(8,128)S(1)} %bitcast.22), custom_call_target="tpu_custom_call" | custom-call | tf_op jit(solution)/shard_map/prepare/pallas_call | solution.py:587
  24.2 0.2 collective-permute-done
  24.5 0.0 copy-done
  24.5 0.0 copy-done.1
  24.5 0.0 copy-done.2
  24.5 23.3 %conditional.1 = (f32[1,3,64,128]{3,2,1,0:T(8,128)S(1)}) conditional(s32[]{:T(128)} %clamp.3, (f32[64,8,128]{2,1,0:T(8,128)S(1)}, s32[1,64]{1,0:T(1,128)S(1)}, s32[1,64]{1,0:T(1,128)S(1)}, f32[3,64,128]{2,1,0:T(8,128)S(1)}, f32[1,3,64,128]{3,2,1,0:T(8,128)S(1)}, /*index=5*/f32[1,2,64,128]{3,2,1,0:T(8,128)S(1)}, ...), branch_computations={%region_0.1_spmd, %region_1.2_spmd, %region_2.3_spmd} | conditional | bytes 1572872 | solution.py:599
  24.5 0.9 %compact_tiles.2 = f32[1024,128]{1,0:T(8,128)S(1)} custom-call(s32[1,64]{1,0:T(1,128)S(1)} %get-tuple-element.50.place_ref, s32[1,64]{1,0:T(1,128)S(1)} %get-tuple-element.52.host_ref, f32[3,64,128]{2,1,0:T(8,128)S(1)} %get-tuple-element.56.halo_ref, f32[512,128]{1,0:T(8,128)S(1)} %bitcast.24), custom_call_target="tpu_custom_call" | custom-call | tf_op jit(solution)/shard_map/cond/branch_0_fun/compact_tiles/pallas_call | solution.py:528
  25.4 17.9 %all_to_all.17 = f32[64,16,128]{2,1,0:T(8,128)S(1)} all-to-all(f32[64,16,128]{2,1,0:T(8,128)S(1)} %bitcast.18), channel_id=1, replica_groups=mesh['sec'=2,'row'=8,'nest'=8] {'row','nest'}, dimensions={0} | all-to-all | bytes 1048576 | tf_op jit(solution)/shard_map/cond/branch_0_fun/all_to_all | solution.py:537
  43.3 4.3 %window_tiles.2 = f32[1,3,64,128]{3,2,1,0:T(8,128)S(1)} custom-call(s32[1,64]{1,0:T(1,128)S(1)} %get-tuple-element.50.place_ref, s32[1,64]{1,0:T(1,128)S(1)} %get-tuple-element.52.host_ref, f32[1,3,64,128]{3,2,1,0:T(8,128)S(1)} %get-tuple-element.53.state_ref, f32[1,2,64,128]{3,2,1,0:T(8,128)S(1)} %get-tuple-element.54.depth_ref, ...), custom_call_target="tpu_custom_call" | custom-call | tf_op jit(solution)/shard_map/cond/branch_0_fun/window_tiles/pallas_call | solution.py:544
  47.8 0.0 copy-start.3
  47.8 0.6 %copy-done.3 = f32[1,3,64,128]{3,2,1,0:T(8,128)} copy-done((f32[1,3,64,128]{3,2,1,0:T(8,128)}, f32[1,3,64,128]{3,2,1,0:T(8,128)S(1)}, u32[]{:S(2)}) %copy-start.3) | copy-done | bytes 98328
Async XLA Ops:
  22.9 1.5 %collective-permute-start = (f32[64,8,128]{2,1,0:T(8,128)S(1)}, f32[64,8,128]{2,1,0:T(8,128)S(1)}, u32[]{:S(2)}, u32[]{:S(2)}) collective-permute-start(f32[64,8,128]{2,1,0:T(8,128)S(1)} %all_to_all.20), channel_id=1, source_target_pairs={{0,64},{64,0},{1,65},{65,1},{2,66},{66,2},{3,67},{67,3},{4,68},{68... | collective-permute-start | bytes 786440 | tf_op jit(solution)/shard_map/ppermute | solution.py:586
  22.9 1.5 %copy-start = (f32[1,3,64,128]{3,2,1,0:T(8,128)S(1)}, f32[1,3,64,128]{3,2,1,0:T(8,128)}, u32[]{:S(2)}) copy-start(f32[1,3,64,128]{3,2,1,0:T(8,128)} %state_in.1) | copy-start | bytes 294916
  22.9 1.5 %copy-start.1 = (f32[1,2,64,128]{3,2,1,0:T(8,128)S(1)}, f32[1,2,64,128]{3,2,1,0:T(8,128)}, u32[]{:S(2)}) copy-start(f32[1,2,64,128]{3,2,1,0:T(8,128)} %depth_in.1) | copy-start | bytes 196612
  22.9 1.5 %copy-start.2 = (s32[1,2,64,128]{3,2,1,0:T(8,128)S(1)}, s32[1,2,64,128]{3,2,1,0:T(8,128)}, u32[]{:S(2)}) copy-start(s32[1,2,64,128]{3,2,1,0:T(8,128)} %open_in.1) | copy-start | bytes 196612
  47.8 0.6 %copy-start.3 = (f32[1,3,64,128]{3,2,1,0:T(8,128)}, f32[1,3,64,128]{3,2,1,0:T(8,128)S(1)}, u32[]{:S(2)}) copy-start(f32[1,3,64,128]{3,2,1,0:T(8,128)S(1)} %get-tuple-element.88) | copy-start | bytes 294916

commit v7 on v6

--- a/solution.py
+++ b/solution.py
@@ -55,8 +55,8 @@
         pltpu.make_async_copy(source, target, sems.at[i])
         for i, (source, target) in enumerate(
             (
+                (state_in, state_ref), (depth_in, depth_ref), (open_in, open_ref),
                 (place_in, place_ref), (host_in, host_ref),
-                (state_in, state_ref), (depth_in, depth_ref), (open_in, open_ref),
             )
         )
     ]

time: 48.7 us -> 48.6 us (level)
  no operation moved by 1% of the time
where the time goes in v7:
time: 48.6 us; the launch traced here: 48.4 us
  blocking collectives  39.7 us (82%)
  Pallas kernels  6.9 us (14%)
  between operations  0.69 us (1%)
  local copies, waits for them, and re-layouts  0.65 us (1%)
    all_to_all x1, blocking collectives, on_device(): lax.all_to_all(packed.reshape(PEERS, 8, COLS), tiles, split_axis=0, conca...  21.8 us
    all_to_all x1, blocking collectives, window(): lax.all_to_all(blocks.reshape(PEERS, block, COLS), ('row', 'nest'), split...  17.9 us
    pallas_call x1, Pallas kernels, window(): pl.pallas_call(functools.partial(window_kernel, tile_side, units), out_sh...  4.31 us
    pallas_call x1, Pallas kernels, on_device(): pl.pallas_call(pack_kernel, out_shape=(jax.ShapeDtypeStruct((PEERS * 8, C...  1.08 us
  transfers between devices with their start and end apart: 1, of which 1 were waited for; matrix products, arithmetic and copies ran while one was open for 0% of the time, Pallas kernels for 1%

profile of v7, /device:TPU:0, one launch (start us, length us, event | category | flops | bytes accessed | tf_op | source)
XLA Modules:
  0.0 48.4 jit_solution(17881375208578049486)
XLA Ops:
  0.0 1.1 %pack.1 = (f32[512,128]{1,0:T(8,128)S(1)}, s32[1,64]{1,0:T(1,128)S(1)}, s32[1,64]{1,0:T(1,128)S(1)}) custom-call(s32[1,64]{1,0:T(1,128)} %bitcast.27, s32[1,64]{1,0:T(1,128)} %bitcast.28, f32[1,3,64,128]{3,2,1,0:T(8,128)} %state_in.1, f32[1,2,64,128]{3,2,1,0:T(8,128)} %depth_in.1, s32[1,2,64,128]{3,2,1,0:T(8,128)} %open_in.1), custom_call_target="tpu_custom_call" | custom-call | tf_op jit(solution)/shard_map/pack/pallas_call | solution.py:562
  1.1 21.8 %all_to_all.20 = f32[64,8,128]{2,1,0:T(8,128)S(1)} all-to-all(f32[64,8,128]{2,1,0:T(8,128)S(1)} %bitcast.21), channel_id=1, replica_groups=mesh['sec'=2,'row'=8,'nest'=8] {'row','nest'}, dimensions={0} | all-to-all | bytes 524288 | tf_op jit(solution)/shard_map/all_to_all | solution.py:583
  22.9 0.0 collective-permute-start
  22.9 0.0 copy-start
  22.9 0.0 copy-start.1
  22.9 0.0 copy-start.2
  22.9 0.6 %prepare.1 = (s32[1,1]{1,0:T(1,128)}, f32[3,64,128]{2,1,0:T(8,128)S(1)}) custom-call(s32[1,64]{1,0:T(1,128)S(1)} %get-tuple-element.77.place_ref, f32[512,128]{1,0:T(8,128)S(1)} %bitcast.22), custom_call_target="tpu_custom_call" | custom-call | tf_op jit(solution)/shard_map/prepare/pallas_call | solution.py:587
  24.2 0.2 collective-permute-done
  24.4 0.0 copy-done
  24.4 0.0 copy-done.1
  24.4 0.0 copy-done.2
  24.4 23.3 %conditional.1 = (f32[1,3,64,128]{3,2,1,0:T(8,128)S(1)}) conditional(s32[]{:T(128)} %clamp.3, (f32[64,8,128]{2,1,0:T(8,128)S(1)}, s32[1,64]{1,0:T(1,128)S(1)}, s32[1,64]{1,0:T(1,128)S(1)}, f32[3,64,128]{2,1,0:T(8,128)S(1)}, f32[1,3,64,128]{3,2,1,0:T(8,128)S(1)}, /*index=5*/f32[1,2,64,128]{3,2,1,0:T(8,128)S(1)}, ...), branch_computations={%region_0.1_spmd, %region_1.2_spmd, %region_2.3_spmd} | conditional | bytes 1572872 | solution.py:599
  24.5 0.9 %compact_tiles.2 = f32[1024,128]{1,0:T(8,128)S(1)} custom-call(s32[1,64]{1,0:T(1,128)S(1)} %get-tuple-element.50.place_ref, s32[1,64]{1,0:T(1,128)S(1)} %get-tuple-element.52.host_ref, f32[3,64,128]{2,1,0:T(8,128)S(1)} %get-tuple-element.56.halo_ref, f32[512,128]{1,0:T(8,128)S(1)} %bitcast.24), custom_call_target="tpu_custom_call" | custom-call | tf_op jit(solution)/shard_map/cond/branch_0_fun/compact_tiles/pallas_call | solution.py:528
  25.4 17.9 %all_to_all.17 = f32[64,16,128]{2,1,0:T(8,128)S(1)} all-to-all(f32[64,16,128]{2,1,0:T(8,128)S(1)} %bitcast.18), channel_id=1, replica_groups=mesh['sec'=2,'row'=8,'nest'=8] {'row','nest'}, dimensions={0} | all-to-all | bytes 1048576 | tf_op jit(solution)/shard_map/cond/branch_0_fun/all_to_all | solution.py:537
  43.2 4.3 %window_tiles.2 = f32[1,3,64,128]{3,2,1,0:T(8,128)S(1)} custom-call(s32[1,64]{1,0:T(1,128)S(1)} %get-tuple-element.50.place_ref, s32[1,64]{1,0:T(1,128)S(1)} %get-tuple-element.52.host_ref, f32[1,3,64,128]{3,2,1,0:T(8,128)S(1)} %get-tuple-element.53.state_ref, f32[1,2,64,128]{3,2,1,0:T(8,128)S(1)} %get-tuple-element.54.depth_ref, ...), custom_call_target="tpu_custom_call" | custom-call | tf_op jit(solution)/shard_map/cond/branch_0_fun/window_tiles/pallas_call | solution.py:544
  47.8 0.0 copy-start.3
  47.8 0.6 %copy-done.3 = f32[1,3,64,128]{3,2,1,0:T(8,128)} copy-done((f32[1,3,64,128]{3,2,1,0:T(8,128)}, f32[1,3,64,128]{3,2,1,0:T(8,128)S(1)}, u32[]{:S(2)}) %copy-start.3) | copy-done | bytes 98328
Async XLA Ops:
  22.9 1.5 %collective-permute-start = (f32[64,8,128]{2,1,0:T(8,128)S(1)}, f32[64,8,128]{2,1,0:T(8,128)S(1)}, u32[]{:S(2)}, u32[]{:S(2)}) collective-permute-start(f32[64,8,128]{2,1,0:T(8,128)S(1)} %all_to_all.20), channel_id=1, source_target_pairs={{0,64},{64,0},{1,65},{65,1},{2,66},{66,2},{3,67},{67,3},{4,68},{68... | collective-permute-start | bytes 786440 | tf_op jit(solution)/shard_map/ppermute | solution.py:586
  22.9 1.5 %copy-start = (f32[1,3,64,128]{3,2,1,0:T(8,128)S(1)}, f32[1,3,64,128]{3,2,1,0:T(8,128)}, u32[]{:S(2)}) copy-start(f32[1,3,64,128]{3,2,1,0:T(8,128)} %state_in.1) | copy-start | bytes 294916
  22.9 1.5 %copy-start.1 = (f32[1,2,64,128]{3,2,1,0:T(8,128)S(1)}, f32[1,2,64,128]{3,2,1,0:T(8,128)}, u32[]{:S(2)}) copy-start(f32[1,2,64,128]{3,2,1,0:T(8,128)} %depth_in.1) | copy-start | bytes 196612
  22.9 1.5 %copy-start.2 = (s32[1,2,64,128]{3,2,1,0:T(8,128)S(1)}, s32[1,2,64,128]{3,2,1,0:T(8,128)}, u32[]{:S(2)}) copy-start(s32[1,2,64,128]{3,2,1,0:T(8,128)} %open_in.1) | copy-start | bytes 196612
  47.8 0.6 %copy-start.3 = (f32[1,3,64,128]{3,2,1,0:T(8,128)}, f32[1,3,64,128]{3,2,1,0:T(8,128)S(1)}, u32[]{:S(2)}) copy-start(f32[1,3,64,128]{3,2,1,0:T(8,128)S(1)} %get-tuple-element.88) | copy-start | bytes 294916
